TPU v7x, 32 devices: a whole 2x2x4 slice. The times are simulated.
32 devices in a mesh: feat: 4 (over y, x), seq: 8 (over z, core).
Axes of the slice: x: 2, y: 2, z: 4, core: 2. Of those that a mesh axis runs over, the one named last changes fastest.
Arguments:
- tokens: bfloat16 [4096, 8192], P('seq', 'feat'), may hold values from -6 to 6
- block_weights: bfloat16 [28672, 512], P('feat'), may hold values from -0.25 to 0.25
- left_factor: bfloat16 [28672, 256], P('feat'), may hold values from -0.09375 to 0.09375
- right_factor: bfloat16 [8192, 256], P('feat'), may hold values from -0.0625 to 0.0625
- pattern: int32 [224, 4], P('feat'), may hold values from 0 to 63, as said below
- cotangent: bfloat16 [4096, 28672], P('seq', 'feat'), may hold values from -6 to 6
Outputs:
- activated: bfloat16 [4096, 28672], P('seq', 'feat')
- grad_input: bfloat16 [8, 512, 8192], P('seq', 'feat')
- grad_blocks: float32 [28672, 512], P(('feat', 'seq'))
- grad_left: float32 [28672, 256], P(('feat', 'seq'))
- grad_right: float32 [8192, 256], P(('feat', 'seq'))
Inputs may be any that keep to these rules, and one draw needn't show every extreme that they name: For block row f, pattern[f, 0] // 8 equals (f * 8) // 224, and pattern[f, j] = pattern[f, 0] XOR ((64) >> j) for 1 <= j < 4.
All inputs are finite; a program needn't handle non-finite values.
Results may differ from a plain program's by a relative error of at most 0.0051.
Values may be sent and summed in bfloat16 or wider, within the bound.
No kernel may reach another device: no remote copies, remote signals or barrier semaphores. Data moves between devices by JAX's collectives and lax.ppermute only.
A program may use at most 256 MiB of HBM per device.

v0:
```python
import math

import jax
import jax.numpy as jnp
from jax import lax
from jax.sharding import PartitionSpec as P

BLK = 128
LEVELS = 4


def from_partner(value, axis, distance):
    mask = 2**distance
    pairs = [(source, source ^ mask) for source in range(lax.axis_size(axis))]
    return lax.ppermute(value, axis, pairs)


def activation(values):
    return jax.nn.gelu(values, approximate=True)


def partner_bit(stride, local_blocks):
    if stride < local_blocks:
        return -1
    return (stride // local_blocks).bit_length() - 1


def local(tokens, block_weights, left_factor, right_factor, pattern, cotangent):
    tok_rows, local_width = tokens.shape
    feat_count = lax.axis_size("feat")
    seq_count = lax.axis_size("seq")
    norm_scale = 1.0 / math.sqrt(tok_rows * seq_count)
    local_blocks = local_width // BLK
    all_blocks = local_blocks * feat_count
    row_blocks = pattern.shape[0]
    out_rows = block_weights.shape[0]
    weight_blocks = block_weights.reshape(row_blocks, BLK, LEVELS, BLK)
    strides = [0] + [all_blocks >> level for level in range(1, LEVELS)]
    pieces = []
    for level in range(LEVELS):
        bit_index = partner_bit(strides[level], local_blocks) if level > 0 else -1
        source = tokens if bit_index < 0 else from_partner(tokens, "feat", bit_index)
        local_ids = pattern[:, level] % local_blocks
        pieces.append(jnp.take(source.reshape(tok_rows, local_blocks, BLK), local_ids, axis=1))
    picked = jnp.stack(pieces, axis=2)
    sparse = jnp.einsum("tfli,foli->tfo", picked, weight_blocks, preferred_element_type=jnp.float32)
    latent_part = jnp.dot(tokens, right_factor, preferred_element_type=jnp.float32)
    latent = lax.psum(latent_part, "feat").astype(jnp.bfloat16)
    pre = sparse.reshape(tok_rows, out_rows) + jnp.einsum(
        "tr,or->to", latent, left_factor, preferred_element_type=jnp.float32
    )
    activated, slope = jax.vjp(activation, pre)
    grad_pre = slope(cotangent.astype(jnp.float32))[0].astype(jnp.bfloat16)
    back_part = jnp.einsum("to,or->tr", grad_pre, left_factor, preferred_element_type=jnp.float32)
    back_latent = lax.psum(back_part, "feat").astype(jnp.bfloat16)
    low_rank = jnp.einsum(
        "tr,ir->ti", back_latent, right_factor, preferred_element_type=jnp.float32
    )
    grad_rows = grad_pre.reshape(tok_rows, row_blocks, BLK)
    spread = jnp.einsum(
        "tfo,foli->tfli", grad_rows, weight_blocks, preferred_element_type=jnp.float32
    )
    summed_grad = low_rank
    for level in range(LEVELS):
        bit_index = partner_bit(strides[level], local_blocks) if level > 0 else -1
        local_ids = pattern[:, level] % local_blocks
        level_term = (
            jnp.zeros((tok_rows, local_blocks, BLK), jnp.float32)
            .at[:, local_ids, :]
            .add(spread[:, :, level, :])
        )
        level_term = level_term.reshape(tok_rows, local_width)
        if bit_index >= 0:
            level_term = from_partner(level_term, "feat", bit_index)
        summed_grad = summed_grad + level_term
    local_grad = summed_grad.astype(jnp.bfloat16)
    regrouped = lax.all_to_all(local_grad, "feat", split_axis=0, concat_axis=1, tiled=True)
    grad_input = regrouped.reshape(1, tok_rows // feat_count, feat_count * local_width)
    window = min(out_rows // seq_count * lax.axis_size("seq") // BLK + 2, row_blocks)
    product = jnp.einsum("tfo,tfli->foli", grad_rows, picked, preferred_element_type=jnp.float32)
    product = product.reshape(window * BLK, LEVELS * BLK) * norm_scale
    grad_blocks = lax.psum_scatter(product, "seq", scatter_dimension=0, tiled=True)
    left_term = (
        jnp.einsum("to,tr->or", grad_pre, latent, preferred_element_type=jnp.float32) * norm_scale
    )
    right_term = (
        jnp.einsum("ti,tr->ir", tokens, back_latent, preferred_element_type=jnp.float32)
        * norm_scale
    )
    grad_left, grad_right = (
        lax.psum_scatter(left_term, "seq", scatter_dimension=0, tiled=True),
        lax.psum_scatter(right_term, "seq", scatter_dimension=0, tiled=True),
    )
    return (activated.astype(jnp.bfloat16), grad_input, grad_blocks, grad_left, grad_right)


def solution(mesh):
    in_specs = (
        P("seq", "feat"),
        P("feat", None),
        P("feat", None),
        P("feat", None),
        P("feat", None),
        P("seq", "feat"),
    )
    out_specs = (
        P("seq", "feat"),
        P("seq", "feat", None),
        P(("feat", "seq"), None),
        P(("feat", "seq"), None),
        P(("feat", "seq"), None),
    )
    return jax.shard_map(local, mesh=mesh, in_specs=in_specs, out_specs=out_specs, check_vma=False)
```

profile of v0, /device:TPU:0, one launch (start us, length us, event | category | flops | bytes accessed | tf_op | source)
XLA Modules:
  0.0 563.2 jit_solution(1598255208283200996)
XLA Ops:
  7.2 4.0 copy.35
  18.8 5.4 gather_fusion.3
  24.2 5.2 gather_fusion
  29.4 11.3 %reshape.59 = bf16[56,128,4,128]{3,2,1,0:T(4,128)(2,1)} reshape(bf16[7168,512]{1,0:T(8,128)(2,1)} %param.9) | data formatting | bytes 14680064 | tf_op jit(solution)/shard_map/reshape | solution.py:37
  42.2 40.7 %all-reduce.2 = bf16[512,256]{1,0:T(8,128)(2,1)S(1)} all-reduce(f32[512,256]{1,0:T(8,128)} %fusion.35), channel_id=1, replica_groups=mesh['feat'=4,'seq'=8] {'feat'}, use_global_device_ids=true, to_apply=%region_0.2 | all-reduce | flops 131072 | bytes 786432 | tf_op jit(solution)/shard_map/psum | solution.py:48
  90.0 5.3 gather_fusion.2
  95.3 6.9 %gather_fusion.1 = bf16[56,512,128]{2,1,0:T(8,128)(2,1)} fusion(bf16[512,16,128]{2,0,1:T(8,128)(2,1)} %copy.38, s32[1024]{0:T(1024)S(1)} %pad_clamp_fusion.2), kind=kCustom, calls=%fused_computation.1.clone | custom fusion | bytes 14680288 | tf_op jit(solution)/shard_map/jit(_take)/gather | solution.py:44
  102.2 12.3 %select_bitcast_fusion = (bf16[512,56,1,128]{3,0,2,1:T(8,128)(2,1)}, bf16[512,56,1,128]{3,0,2,1:T(8,128)(2,1)}) fusion(bf16[56,512,128]{2,1,0:T(8,128)(2,1)} %gather_fusion.3, pred[56]{0:T(512)(128)(4,1)S(1)} %get-tuple-element.41, bf16[56,512,128]{2,1,0:T(8,128)(2,1)} %gather_fusion.2, pred[56]{0:T(512)(128)(4,1)S(1)} %get-tuple-element.43), kind=kLoop, calls=%fused_computation.33 | loop fusion | flops 7340032 | bytes 29360240 | tf_op jit(solution)/shard_map/stack | solution.py:45
  114.4 9.7 %select_bitcast_fusion.2 = (bf16[512,56,1,128]{3,0,2,1:T(8,128)(2,1)}, bf16[512,56,1,128]{3,0,2,1:T(8,128)(2,1)}) fusion(bf16[56,512,128]{2,1,0:T(8,128)(2,1)S(1)} %copy-done.1, pred[56]{0:T(512)(128)(4,1)S(1)} %get-tuple-element.39, bf16[56,512,128]{2,1,0:T(8,128)(2,1)} %gather_fusion, pred[56]{0:T(512)(128)(4,1)S(1)} %get-tuple-element.21), kind=kLoop, calls=%fused_computation.35 | loop fusion | flops 7340032 | bytes 29360240 | tf_op jit(solution)/shard_map/stack | solution.py:45
  124.1 18.4 %fusion.11 = f32[56,512,128,1]{1,2,3,0:T(8,128)} fusion(bf16[56,128,4,128]{3,2,1,0:T(4,128)(2,1)S(1)} %bitcast.124, bf16[512,56,1,128]{3,0,2,1:T(8,128)(2,1)} %get-tuple-element.45, bf16[512,56,1,128]{3,0,2,1:T(8,128)(2,1)} %get-tuple-element.46, bf16[512,56,1,128]{3,0,2,1:T(8,128)(2,1)} %get-tuple-element.47, bf16[512,56,1,128]{3,0,2,1:T(8,128)(2,1)} %get-tuple-element.48), kind=kOutput, calls=%fused_computation.38 | convolution fusion | flops 3802136576 | bytes 51380224 | tf_op jit(solution)/shard_map/tfli,foli->tfo/dot_general | solution.py:46
  142.5 14.3 %copy.43 = f32[512,7168]{1,0:T(8,128)} copy(f32[512,7168]{0,1:T(8,128)} %bitcast.126) | data formatting | bytes 29360128 | tf_op jit(solution)/shard_map/reshape | solution.py:49
  156.9 19.8 %fusion.2 = (bf16[512,7168]{1,0:T(8,128)(2,1)}, bf16[512,7168]{1,0:T(8,128)(2,1)}) fusion(bf16[512,7168]{1,0:T(8,128)(2,1)} %param.13, f32[512,7168]{1,0:T(8,128)} %copy.43, bf16[512,256]{1,0:T(8,128)(2,1)S(1)} %all-reduce.2, bf16[7168,256]{1,0:T(8,128)(2,1)} %param.10), kind=kOutput, calls=%fused_computation.16 | convolution fusion | flops 1967128576 | bytes 40632320 | tf_op jit(solution)/shard_map/tr,or->to/dot_general | solution.py:49
  176.6 7.1 %fusion.36 = f32[512,256]{1,0:T(8,128)} fusion(bf16[512,7168]{1,0:T(8,128)(2,1)} %get-tuple-element.33, bf16[7168,256]{1,0:T(8,128)(2,1)} %param.10), kind=kOutput, calls=%fused_computation.108 | convolution fusion | flops 1879048192 | bytes 11534336 | tf_op jit(solution)/shard_map/to,or->tr/dot_general | solution.py:54
  183.8 24.1 %all-reduce.3 = bf16[512,256]{1,0:T(8,128)(2,1)S(1)} all-reduce(f32[512,256]{1,0:T(8,128)} %fusion.36), channel_id=1, replica_groups=mesh['feat'=4,'seq'=8] {'feat'}, use_global_device_ids=true, to_apply=%region_1.3 | all-reduce | flops 131072 | bytes 786432 | tf_op jit(solution)/shard_map/psum | solution.py:55
  210.2 8.2 %copy.66 = bf16[64,8,56,128]{3,2,1,0:T(8,128)(2,1)} copy(bf16[64,8,56,128]{3,1,2,0:T(8,128)(2,1)} %bitcast.128) | data formatting | bytes 14680064
  218.4 12.3 %copy.57 = bf16[512,56,128,1]{0,2,3,1:T(8,128)(2,1)} copy(bf16[512,56,128,1]{2,1,0,3:T(8,128)(2,1)} %bitcast.125) | data formatting | bytes 14680064 | tf_op jit(solution)/shard_map/reshape | solution.py:59
  230.7 19.3 %convolution_multiply_fusion = f32[56,128,4,128]{3,1,2,0:T(8,128)} fusion(bf16[512,56,128,1]{0,2,3,1:T(8,128)(2,1)} %copy.57, bf16[512,56,1,128]{3,0,2,1:T(8,128)(2,1)} %get-tuple-element.45, bf16[512,56,1,128]{3,0,2,1:T(8,128)(2,1)} %get-tuple-element.46, bf16[512,56,1,128]{3,0,2,1:T(8,128)(2,1)} %get-tuple-element.47, ...), kind=kOutput, calls=%fused_computation.31 | convolution fusion | flops 3879206912 | bytes 51380224 | tf_op jit(solution)/shard_map/tfo,tfli->foli/dot_general | solution.py:80
  250.0 14.7 %copy.52 = f32[56,128,4,128]{1,0,3,2:T(8,128)} copy(f32[56,128,4,128]{3,1,2,0:T(8,128)} %convolution_multiply_fusion) | data formatting | bytes 29360128 | tf_op jit(solution)/shard_map/mul | solution.py:81
  264.8 13.6 %copy.77 = f32[64,8,56,128]{3,1,2,0:T(8,128)} copy(f32[64,8,56,128]{3,2,1,0:T(8,128)} %bitcast.122) | data formatting | bytes 29360128
  279.3 8.7 %convolution_multiply_fusion.1 = f32[7168,256]{1,0:T(8,128)} fusion(bf16[512,7168]{1,0:T(8,128)(2,1)} %get-tuple-element.33, bf16[512,256]{1,0:T(8,128)(2,1)S(1)} %copy-done.7), kind=kOutput, calls=%fused_computation.32 | convolution fusion | flops 1880883200 | bytes 14942208 | tf_op jit(solution)/shard_map/to,tr->or/dot_general | solution.py:84
  288.7 26.0 %convolution_bitcast_fusion = f32[512,56,4,128]{3,0,2,1:T(8,128)} fusion(bf16[512,56,128,1]{0,2,3,1:T(8,128)(2,1)} %copy.57, bf16[56,128,4,128]{3,2,1,0:T(4,128)(2,1)} %reshape.59), kind=kOutput, calls=%fused_computation.9 | convolution fusion | flops 3758096384 | bytes 73400320 | tf_op jit(solution)/shard_map/tfo,foli->tfli/dot_general | solution.py:60
  314.6 39.3 %slice_bitcast_fusion.3 = (f32[56,512,128]{2,1,0:T(8,128)}, f32[56,512,128]{2,1,0:T(8,128)}, f32[56,512,128]{2,1,0:T(8,128)}, f32[56,512,128]{2,1,0:T(8,128)}) fusion(f32[512,56,4,128]{3,0,2,1:T(8,128)} %convolution_bitcast_fusion), kind=kLoop, calls=%fused_computation.28 | loop fusion | bytes 117440512 | tf_op jit(solution)/shard_map/squeeze | solution.py:70
  356.3 31.3 %scatter_fusion.1 = f32[512,16,128]{2,0,1:T(8,128)} fusion(f32[512,16,128]{2,0,1:T(8,128)} %broadcast.83.clone.1, s32[56]{0:T(128)S(1)} %get-tuple-element.36, f32[56,512,128]{2,1,0:T(8,128)} %get-tuple-element.32), kind=kCustom, calls=%fused_computation.5 | custom fusion | flops 3670016 | bytes 44040416 | tf_op jit(solution)/shard_map/scatter-add | solution.py:70
  387.5 4.8 copy_bitcast_fusion.2
  396.2 31.0 %scatter_fusion.2 = f32[512,16,128]{2,0,1:T(8,128)} fusion(f32[512,16,128]{2,0,1:T(8,128)} %broadcast.83.clone, s32[56]{0:T(128)S(1)} %get-tuple-element.37, f32[56,512,128]{2,1,0:T(8,128)} %get-tuple-element.31), kind=kCustom, calls=%fused_computation.6 | custom fusion | flops 3670016 | bytes 44040416 | tf_op jit(solution)/shard_map/scatter-add | solution.py:70
  427.2 4.8 copy_bitcast_fusion.1
  435.8 31.5 %scatter_fusion = f32[512,16,128]{2,0,1:T(8,128)} fusion(f32[512,16,128]{2,0,1:T(8,128)} %broadcast.83.clone.3, s32[56]{0:T(128)S(1)} %get-tuple-element.35, f32[56,512,128]{2,1,0:T(8,128)} %get-tuple-element.29), kind=kCustom, calls=%fused_computation.4 | custom fusion | flops 3670016 | bytes 44040416 | tf_op jit(solution)/shard_map/scatter-add | solution.py:70
  469.8 31.4 %scatter_fusion.3 = f32[512,16,128]{2,0,1:T(8,128)} fusion(f32[512,16,128]{2,0,1:T(8,128)} %broadcast.83.clone.2, s32[56]{0:T(128)S(1)} %get-tuple-element.38, f32[56,512,128]{2,1,0:T(8,128)} %get-tuple-element.30), kind=kCustom, calls=%fused_computation.7 | custom fusion | flops 3670016 | bytes 44040416 | tf_op jit(solution)/shard_map/scatter-add | solution.py:70
  501.2 16.0 %collective-permute-done.3 = f32[512,2048]{1,0:T(8,128)} collective-permute-done((f32[512,2048]{1,0:T(8,128)}, f32[512,2048]{1,0:T(8,128)}, u32[]{:S(2)}, u32[]{:S(2)}) %collective-permute-start.3) | collective-permute-done | bytes 4194336 | tf_op jit(solution)/shard_map/ppermute | solution.py:15
  517.3 8.3 %fusion.13 = bf16[512,2048]{1,0:T(8,128)(2,1)} fusion(f32[512,2048]{1,0:T(8,128)} %collective-permute-done.3, f32[512,2048]{1,0:T(8,128)} %collective-permute-done.2, bf16[2048,256]{1,0:T(8,128)(2,1)S(1)} %copy-done, bf16[512,256]{1,0:T(8,128)(2,1)S(1)} %copy-done.5, f32[512,16,128]{2,0,1:T(8,128)} %scatter_fusion.3, f32[512,16,128]{2,0,1:T(8,128)} %scatter_fusion), kind=kOutput, calls=%fused_computation.41 | convolution fusion | flops 542113792 | bytes 20185088 | tf_op jit(solution)/shard_map/tr,ir->ti/dot_general | solution.py:56
  531.3 15.0 %all-to-all-done = bf16[4,128,2048]{2,1,0:T(8,128)(2,1)S(1)} async-done(((bf16[4,128,2048]{2,1,0:T(8,128)(2,1)}), bf16[4,128,2048]{2,1,0:T(8,128)(2,1)S(1)}, u32[]{:S(2)}, u32[]{:S(2)}) %all-to-all-start) | async-done | bytes 2097184 | tf_op jit(solution)/shard_map/all_to_all | solution.py:77
  549.2 4.4 reshape.66
  (60 shorter events, 43.9 us)
Async XLA Ops:
  7.2 33.6 %copy-start = (bf16[2048,256]{1,0:T(8,128)(2,1)S(1)}, bf16[2048,256]{1,0:T(8,128)(2,1)}, u32[]{:S(2)}) copy-start(bf16[2048,256]{1,0:T(8,128)(2,1)} %param.11) | copy-start | bytes 3145732
  7.2 11.6 %copy-start.8 = (s32[56,4]{0,1:T(4,128)S(1)}, s32[56,4]{0,1:T(4,128)}, u32[]{:S(2)}) copy-start(s32[56,4]{0,1:T(4,128)} %param.12) | copy-start | bytes 2692
  7.2 522.3 %reduce-scatter.8.cloned.1.call-start = ((), (), s32[]{:S(2)}) async-start(), calls=%async_computation.6 | async-start | bytes 2359296 | tf_op jit(solution)/shard_map/reduce_scatter | solution.py:92
  11.2 71.7 %collective-permute-start.1 = (bf16[512,2048]{0,1:T(8,128)(2,1)}, bf16[512,2048]{0,1:T(8,128)(2,1)}, u32[]{:S(2)}, u32[]{:S(2)}) collective-permute-start(bf16[512,2048]{0,1:T(8,128)(2,1)} %copy.35), channel_id=1, source_target_pairs={{0,8},{8,0},{16,24},{24,16},{1,9},{9,1},{17,25},{25,17},{2,10},{10... | collective-permute-start | bytes 6291464 | tf_op jit(solution)/shard_map/ppermute | solution.py:15
  14.2 71.9 %collective-permute-start = (bf16[512,2048]{0,1:T(8,128)(2,1)}, bf16[512,2048]{0,1:T(8,128)(2,1)}, u32[]{:S(2)}, u32[]{:S(2)}) collective-permute-start(bf16[512,2048]{0,1:T(8,128)(2,1)} %copy.35), channel_id=1, source_target_pairs={{0,16},{8,24},{16,0},{24,8},{1,17},{9,25},{17,1},{25,9},{2,18},{10... | collective-permute-start | bytes 6291464 | tf_op jit(solution)/shard_map/ppermute | solution.py:15
  29.4 11.3 %copy-start.2 = (bf16[512,2048]{1,0:T(8,128)(2,1)S(1)}, bf16[512,2048]{1,0:T(8,128)(2,1)}, u32[]{:S(2)}) copy-start(bf16[512,2048]{1,0:T(8,128)(2,1)} %param.8) | copy-start | bytes 6291460
  83.0 73.9 %copy-start.6 = (bf16[512,256]{1,0:T(8,128)(2,1)}, bf16[512,256]{1,0:T(8,128)(2,1)S(1)}, u32[]{:S(2)}) copy-start(bf16[512,256]{1,0:T(8,128)(2,1)S(1)} %all-reduce.2) | copy-start | bytes 786436
  102.2 12.3 %copy-start.1 = (bf16[56,512,128]{2,1,0:T(8,128)(2,1)S(1)}, bf16[56,512,128]{2,1,0:T(8,128)(2,1)}, u32[]{:S(2)}) copy-start(bf16[56,512,128]{2,1,0:T(8,128)(2,1)} %gather_fusion.1) | copy-start | bytes 22020100
  102.2 21.9 %slice-start = ((s8[7340032]{0:T(1024)(128)(4,1)}), s8[4194304]{0:T(1024)(128)(4,1)S(1)}, s32[]{:S(2)}) async-start(s8[7340032]{0:T(1024)(128)(4,1)} %bitcast.123), calls=%async_computation.7 | async-start | bytes 8388608
  114.4 9.7 %slice-start.1 = ((s8[7340032]{0:T(1024)(128)(4,1)}), s8[3145728]{0:T(1024)(128)(4,1)S(1)}, s32[]{:S(2)}) async-start(s8[7340032]{0:T(1024)(128)(4,1)} %bitcast.123), calls=%async_computation.8 | async-start | bytes 6291456
  176.6 31.3 %copy-start.3 = (bf16[512,2048]{1,0:T(8,128)(2,1)S(1)}, bf16[512,2048]{1,0:T(8,128)(2,1)}, u32[]{:S(2)}) copy-start(bf16[512,2048]{1,0:T(8,128)(2,1)} %param.8) | copy-start | bytes 6291460
  207.9 10.5 %copy-start.4 = (bf16[512,256]{1,0:T(8,128)(2,1)}, bf16[512,256]{1,0:T(8,128)(2,1)S(1)}, u32[]{:S(2)}) copy-start(bf16[512,256]{1,0:T(8,128)(2,1)S(1)} %all-reduce.3) | copy-start | bytes 786436
  210.0 343.7 %reduce-scatter.4.cloned.1.call-start = ((), (), s32[]{:S(2)}) async-start(), calls=%async_computation.4 | async-start | bytes 16515072 | tf_op jit(solution)/shard_map/reduce_scatter | solution.py:82
  278.3 0.9 copy-start.7
  278.4 278.0 %reduce-scatter.6.cloned.1.call-start = ((), (), s32[]{:S(2)}) async-start(), calls=%async_computation.5 | async-start | bytes 8257536 | tf_op jit(solution)/shard_map/reduce_scatter | solution.py:91
  288.0 0.7 copy-start.9
  392.4 108.9 %collective-permute-start.2 = (f32[512,2048]{1,0:T(8,128)}, f32[512,2048]{1,0:T(8,128)}, u32[]{:S(2)}, u32[]{:S(2)}) collective-permute-start(f32[512,2048]{1,0:T(8,128)} %copy_bitcast_fusion.2), channel_id=1, source_target_pairs={{0,16},{8,24},{16,0},{24,8},{1,17},{9,25},{17,1},{25,9},{2,18},{10... | collective-permute-start | bytes 12582920 | tf_op jit(solution)/shard_map/ppermute | solution.py:15
  432.0 85.2 %collective-permute-start.3 = (f32[512,2048]{1,0:T(8,128)}, f32[512,2048]{1,0:T(8,128)}, u32[]{:S(2)}, u32[]{:S(2)}) collective-permute-start(f32[512,2048]{1,0:T(8,128)} %copy_bitcast_fusion.1), channel_id=1, source_target_pairs={{0,8},{8,0},{16,24},{24,16},{1,9},{9,1},{17,25},{25,17},{2,10},{10... | collective-permute-start | bytes 12582920 | tf_op jit(solution)/shard_map/ppermute | solution.py:15
  469.8 47.5 %copy-start.5 = (bf16[512,256]{1,0:T(8,128)(2,1)S(1)}, bf16[512,256]{1,0:T(8,128)(2,1)}, u32[]{:S(2)}) copy-start(bf16[512,256]{1,0:T(8,128)(2,1)} %copy-done.4) | copy-start | bytes 786436
  525.6 20.7 %all-to-all-start = ((bf16[4,128,2048]{2,1,0:T(8,128)(2,1)}), bf16[4,128,2048]{2,1,0:T(8,128)(2,1)S(1)}, u32[]{:S(2)}, u32[]{:S(2)}) async-start(bf16[4,128,2048]{2,1,0:T(8,128)(2,1)} %bitcast.33), calls=%async_computation | async-start | bytes 4194304 | tf_op jit(solution)/shard_map/all_to_all | solution.py:77
Sparse Core Ops, SparseCore 0:
  210.1 36.4 reduce-scatter.7
  278.5 149.6 reduce-scatter.3
  431.1 78.0 reduce-scatter.5
where the time goes:
time: 569 us; the launch traced here: 563 us
  local copies, waits for them, and re-layouts  183 us (32%)
  other arithmetic  147 us (26%)
  matrix products  111 us (20%)
  blocking collectives  64.8 us (11%)
  waiting for transfers between devices  31.1 us (5%)
  between operations  14.2 us (2%)
  starting transfers between devices  11.4 us (2%)
    scatter-add x4, other arithmetic, local(): level_term = jnp.zeros((tok_rows, local_blocks, BLK), jnp.float32).at[:,...  125 us
    psum x1, blocking collectives, local(): latent = lax.psum(latent_part, 'feat').astype(jnp.bfloat16)  40.7 us
    squeeze x1, local copies, waits for them, and re-layouts, local(): spread[:, :, level, :]  39.3 us
    unnamed x29, local copies, waits for them, and re-layouts  31.8 us
    dot_general x1, matrix products, local(): jnp.einsum('tfo,foli->tfli', grad_rows, weight_blocks, preferred_element_...  26 us
    psum x1, blocking collectives, local(): back_latent = lax.psum(back_part, 'feat').astype(jnp.bfloat16)  24.1 us
    gather x4, local copies, waits for them, and re-layouts, local(): jnp.take(source.reshape(tok_rows, local_blocks, BLK), local_ids, axis=1)  22.7 us
    another operation x2, other arithmetic, local(): picked = jnp.stack(pieces, axis=2)  21.9 us
  transfers between devices with their start and end apart: 8, of which 2 were waited for; matrix products, arithmetic and copies ran while one was open for 60% of the time, Pallas kernels for 0%

commit v1 on v0

v1 whole, which is shorter than its diff:
```python
import functools
import math

import jax
import jax.numpy as jnp
from jax import lax
from jax.experimental import pallas as pl
from jax.experimental.pallas import tpu as pltpu
from jax.sharding import PartitionSpec as P

BLK = 128
LEVELS = 4
GROUPS = 8
STEP = 7
CHUNKS = 4
COST = 30 * 10**9
VMEM = 56 * 1024 * 1024
F32 = jnp.float32
BF16 = jnp.bfloat16
GELU_K = math.sqrt(2.0 / math.pi)
GELU_A = 0.044715


def from_partner(value, axis, distance):
    pairs = [(source, source ^ distance) for source in range(lax.axis_size(axis))]
    return lax.ppermute(value, axis, pairs)


def others(part, axis):
    return [from_partner(part, axis, distance) for distance in range(1, lax.axis_size(axis))]


def forward_kernel(turn, width, pattern_ref, place_ref, *refs):
    slabs = refs[:LEVELS]
    latent_ref, weight_ref, left_ref, cot_ref = refs[LEVELS : LEVELS + 4]
    act_ref, grad_ref, sums_ref, back_ref = refs[-4:]
    step = pl.program_id(0)
    first = chunk_step(place_ref, turn, step) * STEP

    def operands(row):
        column = lax.rem(pattern_ref[first + row, 0], width)
        lanes = pl.ds(pl.multiple_of(column * BLK, BLK), BLK)
        return jnp.concatenate([slab[:, lanes] for slab in slabs] + [latent_ref[...]], axis=1)

    every = [slice(row * BLK, (row + 1) * BLK) for row in range(STEP)]
    pres = []
    for row, rows in enumerate(every):
        weights = jnp.concatenate([weight_ref[rows, :], left_ref[rows, :]], axis=1)
        pres.append(
            lax.dot_general(operands(row), weights, (((1,), (1,)), ((), ())), preferred_element_type=F32)
        )
    grads = []
    for pre, rows in zip(pres, every):
        square = pre * pre
        half = 0.5 + 0.5 * jnp.tanh(pre * (GELU_K + (GELU_K * GELU_A) * square))
        act = pre * half
        act_ref[:, rows] = act.astype(BF16)
        slope = half + act * (1.0 - half) * (2.0 * GELU_K + (6.0 * GELU_K * GELU_A) * square)
        grad = (cot_ref[:, rows].astype(F32) * slope).astype(BF16)
        grad_ref[:, rows] = grad
        grads.append(grad)
    for row, rows in enumerate(every):
        sums_ref[rows, :] = lax.dot_general(
            grads[row], operands(row), (((0,), (0,)), ((), ())), preferred_element_type=F32
        ).astype(BF16)
    back = jnp.dot(jnp.concatenate(grads, axis=1), left_ref[...], preferred_element_type=F32)

    @pl.when(step == 0)
    def _():
        back_ref[...] = back

    @pl.when(step > 0)
    def _():
        back_ref[...] += back


def chunk_step(place, turn, step):
    per_chunk = place[0]
    return place[1 + turn + step // per_chunk] * per_chunk + lax.rem(step, per_chunk)


def chunk_group(place, turn):
    return place[1 + CHUNKS + turn]


def forward_chunk(turn, steps, width, pattern, place, slabs, moves, latent, weights, left, cot, carried, after=()):
    tok_rows, hidden = cot.shape
    rank = left.shape[1]
    wide = STEP * BLK
    rows = steps * wide
    at_slab = lambda move: (lambda i, p, w: (0, 0 if move is None else chunk_group(w, turn) ^ move))
    in_specs = [pl.BlockSpec((tok_rows, width * BLK), at_slab(move)) for move in moves] + [
        pl.BlockSpec((tok_rows, rank), lambda i, p, w: (0, 0)),
        pl.BlockSpec((wide, LEVELS * BLK), lambda i, p, w: (chunk_step(w, turn, i), 0)),
        pl.BlockSpec((wide, rank), lambda i, p, w: (chunk_step(w, turn, i), 0)),
        pl.BlockSpec((tok_rows, wide), lambda i, p, w: (0, chunk_step(w, turn, i))),
    ]
    operands = [pattern, place, *slabs, latent, weights, left, cot]
    aliases = {}
    if carried is not None:
        aliases = {len(operands): 0, len(operands) + 1: 1}
        operands += list(carried)
    operands += list(after)
    in_specs += [pl.BlockSpec(memory_space=pl.ANY)] * (len(operands) - 2 - len(in_specs))
    out_cols = LEVELS * BLK + rank
    return pl.pallas_call(
        functools.partial(forward_kernel, turn, width),
        grid_spec=pltpu.PrefetchScalarGridSpec(
            num_scalar_prefetch=2,
            grid=(steps,),
            in_specs=in_specs,
            out_specs=[
                pl.BlockSpec((tok_rows, wide), lambda i, p, w: (0, chunk_step(w, turn, i))),
                pl.BlockSpec((tok_rows, wide), lambda i, p, w: (0, chunk_step(w, turn, i))),
                pl.BlockSpec((wide, out_cols), lambda i, p, w: (i, 0)),
                pl.BlockSpec((tok_rows, rank), lambda i, p, w: (0, 0)),
            ],
        ),
        out_shape=[
            jax.ShapeDtypeStruct((tok_rows, hidden), BF16),
            jax.ShapeDtypeStruct((tok_rows, hidden), BF16),
            jax.ShapeDtypeStruct((rows, out_cols), BF16),
            jax.ShapeDtypeStruct((tok_rows, rank), F32),
        ],
        input_output_aliases=aliases,
        compiler_params=pltpu.CompilerParams(vmem_limit_bytes=VMEM),
        cost_estimate=pl.CostEstimate(flops=COST, bytes_accessed=24 << 20, transcendentals=0),
        name="forward_chunk",
    )(*operands)


def spread_kernel(turn, steps, width, moves, levels, last, pattern_ref, place_ref, grad_ref, weight_ref, *refs):
    out_ref, total = refs[-2], refs[-1]
    step = pl.program_id(0)
    first = chunk_step(place_ref, turn, step) * STEP
    span = width * BLK

    @pl.when(step == 0)
    def _():
        total[...] = jnp.zeros_like(total)

    weights = weight_ref[...]
    weights = jnp.concatenate([weights[:, level * BLK : (level + 1) * BLK] for level in levels], axis=1)
    for row in range(STEP):
        cols = slice(row * BLK, (row + 1) * BLK)
        column = lax.rem(pattern_ref[first + row, 0], width)
        terms = jnp.dot(grad_ref[:, cols], weights[cols, :], preferred_element_type=F32)
        for at, level in enumerate(levels):
            if last:
                begin = step_group(place_ref, turn, step) ^ moves[level]
            else:
                begin = at
            lanes = pl.ds(pl.multiple_of(begin * span + column * BLK, BLK), BLK)
            total[:, lanes] += terms[:, at * BLK : (at + 1) * BLK]

    @pl.when(step == steps - 1)
    def _():
        value = total[...]
        if last:
            value = value + lax.dot_general(
                refs[0][...], refs[1][...], (((1,), (1,)), ((), ())), preferred_element_type=F32
            )
        out_ref[...] = value.astype(BF16)


def step_group(place, turn, step):
    return place[1 + CHUNKS + turn + step // place[0]]


def spread(turn, steps, width, pattern, place, grad, weights, moves, levels, extra, out_cols, after=()):
    tok_rows = grad.shape[0]
    wide = STEP * BLK
    return pl.pallas_call(
        functools.partial(spread_kernel, turn, steps, width, tuple(moves), tuple(levels), bool(extra)),
        grid_spec=pltpu.PrefetchScalarGridSpec(
            num_scalar_prefetch=2,
            grid=(steps,),
            in_specs=[
                pl.BlockSpec((tok_rows, wide), lambda i, p, w: (0, chunk_step(w, turn, i))),
                pl.BlockSpec((wide, LEVELS * BLK), lambda i, p, w: (chunk_step(w, turn, i), 0)),
            ]
            + [pl.BlockSpec(value.shape, lambda i, p, w: (0, 0)) for value in extra]
            + [pl.BlockSpec(memory_space=pl.ANY)] * len(after),
            out_specs=pl.BlockSpec((tok_rows, out_cols), lambda i, p, w: (0, 0)),
            scratch_shapes=[pltpu.VMEM((tok_rows, out_cols), F32)],
        ),
        out_shape=jax.ShapeDtypeStruct((tok_rows, out_cols), BF16),
        compiler_params=pltpu.CompilerParams(vmem_limit_bytes=VMEM),
        cost_estimate=pl.CostEstimate(flops=COST, bytes_accessed=24 << 20, transcendentals=0),
        name="spread",
    )(pattern, place, grad, weights, *extra, *after)


def merge_kernel(remote, distances, span, place_ref, own_ref, *refs):
    sources, out_ref = refs[:-1], refs[-1]
    owner = pl.program_id(0)
    for turn in range(len(sources)):
        lanes = pl.ds(pl.multiple_of((chunk_group(place_ref, 0) ^ turn) * span, span), span)
        total = own_ref[owner, :, lanes].astype(F32)
        for at, level in enumerate(remote):
            total = total + sources[turn][owner ^ distances[level], :, at * span : (at + 1) * span].astype(F32)
        out_ref[0, :, lanes] = total.astype(BF16)


def merge_terms(place, own, arrived, remote, distances, span):
    count, rows, width = own.shape
    return pl.pallas_call(
        functools.partial(merge_kernel, tuple(remote), tuple(distances), span),
        grid_spec=pltpu.PrefetchScalarGridSpec(
            num_scalar_prefetch=1,
            grid=(count,),
            in_specs=[pl.BlockSpec(value.shape, lambda q, w: (0, 0, 0)) for value in (own, *arrived)],
            out_specs=pl.BlockSpec((1, rows, width), lambda q, w: (0, 0, q)),
        ),
        out_shape=jax.ShapeDtypeStruct((1, rows, count * width), BF16),
        compiler_params=pltpu.CompilerParams(vmem_limit_bytes=VMEM),
        name="merge_terms",
    )(place, own, *arrived)


def right_kernel(bits, rows, place_ref, tokens_ref, back_ref, keep_ref, send_ref):
    even = place_ref[1 + 2 * CHUNKS] == 0
    for turn in range(CHUNKS):
        for pair in range(1 << (bits - 1)):
            begin = ((place_ref[1 + turn] << (bits - 1)) + pair) * 2 * rows
            lanes = pl.ds(pl.multiple_of(begin, 2 * rows), 2 * rows)
            both = lax.dot_general(
                tokens_ref[:, lanes], back_ref[...], (((0,), (0,)), ((), ())), preferred_element_type=F32
            )
            low, high = both[:rows], both[rows:]
            at = slice(pair * rows, (pair + 1) * rows)
            keep_ref[turn, at, :] = jnp.where(even, low, high).astype(BF16)
            send_ref[turn, at, :] = jnp.where(even, high, low).astype(BF16)


def right_sums(bits, count, place, tokens, back):
    rows = tokens.shape[1] // count
    shape = jax.ShapeDtypeStruct((CHUNKS, rows << (bits - 1), back.shape[1]), BF16)
    return pl.pallas_call(
        functools.partial(right_kernel, bits, rows),
        grid_spec=pltpu.PrefetchScalarGridSpec(
            num_scalar_prefetch=1,
            grid=(1,),
            in_specs=[pl.BlockSpec(value.shape, lambda i, w: (0, 0)) for value in (tokens, back)],
            out_specs=[pl.BlockSpec(shape.shape, lambda i, w: (0, 0, 0))] * 2,
        ),
        out_shape=[shape, shape],
        compiler_params=pltpu.CompilerParams(vmem_limit_bytes=VMEM),
        name="right_sums",
    )(place, tokens, back)


def pair_sums(value, other, index, bits):
    count = 1 << bits
    rows = value.shape[0] // count
    split = lambda v: v.reshape(count // 2, 2, rows, v.shape[1])
    mine = lambda v: lax.dynamic_index_in_dim(split(v), index & 1, 1, keepdims=False).astype(F32)
    return lower_sums(mine(value) + mine(other), index, bits)


def lower_sums(part, index, bits):
    for bit in range(1, bits):
        mine = (index >> bit) & 1
        part = part.reshape(part.shape[0] // 2, 2, *part.shape[1:])
        keep = lax.dynamic_index_in_dim(part, mine, 1, keepdims=False)
        send = lax.dynamic_index_in_dim(part, 1 - mine, 1, keepdims=False)
        part = keep + from_partner(send.astype(BF16), "seq", 1 << bit).astype(F32)
    return part[0]


def local(tokens, block_weights, left_factor, right_factor, pattern, cotangent):
    tok_rows, local_width = tokens.shape
    feat_count = lax.axis_size("feat")
    seq_count = lax.axis_size("seq")
    norm_scale = 1.0 / math.sqrt(tok_rows * seq_count)
    local_blocks = local_width // BLK
    width = local_blocks * feat_count // GROUPS
    groups = local_blocks // width
    rows = pattern.shape[0] // groups
    span = width * BLK
    strides = [0] + [GROUPS >> level for level in range(1, LEVELS)]
    distances = [stride // groups for stride in strides]
    moves = [stride if stride < groups else 0 for stride in strides]

    index = lax.axis_index("seq")
    bits = seq_count.bit_length() - 3
    near, far = 1 << bits, 2 << bits
    quarter = index >> bits

    latent_part = jnp.dot(tokens, right_factor, preferred_element_type=F32)
    distance = feat_count // 2
    other = from_partner(latent_part.astype(BF16), "feat", distance)
    tokens_after, other = lax.optimization_barrier((tokens, other))
    received = []
    for turn in range(groups):
        group = (quarter ^ (CHUNKS - 1)) * groups // CHUNKS ^ turn
        piece = lax.dynamic_slice_in_dim(tokens, group * span, span, 1)
        late = lax.dynamic_slice_in_dim(tokens_after, group * span, span, 1)
        sources = [late if turn > 0 or d == feat_count // 2 else piece for d in distances]
        received.append([from_partner(s, "feat", d) if d > 0 else None for s, d in zip(sources, distances)])
        if turn == 0:
            latent_part = latent_part + other.astype(F32)
            while distance > 1:
                distance //= 2
                tokens_after, latent_part = lax.optimization_barrier((tokens_after, latent_part))
                latent_part = latent_part + from_partner(latent_part.astype(BF16), "feat", distance).astype(F32)
    latent = latent_part.astype(BF16)

    remote = [level for level in range(LEVELS) if distances[level] > 0]
    slots = [None if d > 0 else move for d, move in zip(distances, moves)]
    steps = pattern.shape[0] // STEP // CHUNKS
    turns = CHUNKS // groups
    part_rows = tok_rows // feat_count

    def to_owner(value):
        value = value.reshape(feat_count, part_rows, value.shape[1])
        return lax.all_to_all(value, "feat", split_axis=0, concat_axis=0, tiled=True)

    chunks = [quarter ^ (CHUNKS - 1 - turn) for turn in range(CHUNKS)]
    place = jnp.stack([jnp.int32(steps)] + chunks + [chunk * groups // CHUNKS for chunk in chunks] + [index & 1]).astype(jnp.int32)

    def forward(turn, count, carried, after=()):
        slabs = [tokens if slab is None else slab for slab in received[turn // turns]]
        return forward_chunk(
            turn, steps * count, width, pattern, place, slabs, slots, latent, block_weights, left_factor, cotangent,
            carried, after,
        )

    def spread_levels(turn, count, grad, levels, extra, out_cols, after=()):
        return spread(
            turn, steps * count, width, pattern, place, grad, block_weights, moves, levels, extra, out_cols, after
        )

    hold = lax.optimization_barrier
    near_hop = lambda value: from_partner(value, "seq", near)
    far_hop = lambda value: from_partner(value, "seq", far)

    def line_hop(value, routes):
        low = range(near)
        pairs = [(a * near + at, b * near + at) for a, b in routes for at in low]
        return lax.ppermute(value, "seq", pairs)

    inward = lambda value: line_hop(value, [(0, 1), (3, 2)])
    across = lambda value: line_hop(value, [(1, 2), (2, 1)])
    core_hop = lambda value: from_partner(value, "seq", 1)
    wide = lambda value: value.astype(F32)

    act, grad, total0, back0 = forward(0, 1, None)
    swap0 = core_hop(total0)
    act, grad, total1, back1 = forward(1, 1, (act, grad), [slab for slab in received[-1] if slab is not None])
    grad, total1, swap0 = hold((grad, total1, swap0))

    sum0 = pair_sums(total0, swap0, index, bits).astype(BF16)
    got0 = inward(sum0)
    swap1 = core_hop(total1)
    arrived = []
    if groups > 1:
        terms = spread_levels(0, turns, grad, remote, (), len(remote) * span)
        terms, swap1, grad = hold((terms, swap1, grad))
        arrived.append(to_owner(terms))
    sum1 = pair_sums(total1, swap1, index, bits).astype(BF16)
    got1 = inward(sum1)
    act, grad, total2, back2 = forward(2, 1, (act, grad))
    grad, total2, back2, got0 = hold((grad, total2, back2, got0))

    got2 = across((wide(sum1) + wide(got0)).astype(BF16))
    swap2 = core_hop(total2)
    act, grad, total3, back3 = forward(3, 1, (act, grad))
    grad, total3, back3, swap2, arrived = hold((grad, total3, back3, swap2, arrived))

    swap3 = core_hop(total3)
    back = back0 + back1 + back2 + back3
    parts = others(back.astype(BF16), "feat")
    sum2 = pair_sums(total2, swap2, index, bits)
    terms = spread_levels(CHUNKS - turns, turns, grad, remote, (), len(remote) * span)
    terms, swap3, parts, got1, got2, grad = hold((terms, swap3, parts, got1, got2, grad))

    for part in parts:
        back = back + wide(part)
    back_latent = back.astype(BF16)
    got3 = across((wide(sum0) + wide(got1)).astype(BF16))
    got4 = near_hop((sum2 + wide(got2)).astype(BF16))
    arrived.append(to_owner(terms))
    right_keep, right_send = right_sums(bits, seq_count, place, tokens, back_latent)
    right_swap = core_hop(right_send)
    own_levels = [level for level in range(LEVELS) if level not in remote]
    own = spread_levels(0, CHUNKS, grad, own_levels, (back_latent, right_factor), local_width)
    own, right_swap = hold((own, right_swap))

    own = to_owner(own)
    right = wide(right_keep) + wide(right_swap)
    right = jnp.stack(
        [lower_sums(part.reshape(1 << (bits - 1), -1, part.shape[1]), index, bits) for part in right]
    )
    close = near_hop(right[0::2].astype(BF16))
    grad_right = right[3] + wide(close[1]) + wide(far_hop((right[1] + wide(close[0])).astype(BF16)))
    grad_right = grad_right * norm_scale
    final = pair_sums(total3, swap3, index, bits) + wide(got3) + wide(got4)
    final = final * norm_scale
    grad_input = merge_terms(place, own, arrived, remote, distances, span)

    return (act, grad_input, final[:, : LEVELS * BLK], final[:, LEVELS * BLK :], grad_right)


def solution(mesh):
    in_specs = (
        P("seq", "feat"),
        P("feat", None),
        P("feat", None),
        P("feat", None),
        P("feat", None),
        P("seq", "feat"),
    )
    out_specs = (
        P("seq", "feat"),
        P("seq", "feat", None),
        P(("feat", "seq"), None),
        P(("feat", "seq"), None),
        P(("feat", "seq"), None),
    )
    return jax.shard_map(local, mesh=mesh, in_specs=in_specs, out_specs=out_specs, check_vma=False)
```

time: 569 us -> 236 us (0.41)
  local copies, waits for them, and re-layouts: 183 us -> 8.67 us
  other arithmetic: 147 us -> 21.9 us
  matrix products: 111 us -> 2.72 us
  Pallas kernels: 0 us -> 103 us
  blocking collectives: 64.8 us -> 0 us
  starting transfers between devices: 11.4 us -> 45.4 us
  waiting for transfers between devices: 31.1 us -> 51.8 us
  between operations: 14.2 us -> 0.94 us
    scatter-add x4 -> x0, other arithmetic: 125 us -> none  [local(): level_term = jnp.zeros((tok_rows, local_blocks, BLK), jnp.float32).at[:,...]
    dot_general x9 -> x1, matrix products: 111 us -> 2.72 us  [local(): latent_part = jnp.dot(tokens, right_factor, preferred_element_type=F32)]
    pallas_call x0 -> x9, Pallas kernels: none -> 103 us  [the longest x4 57.6 us: forward_chunk(): pl.pallas_call(functools.partial(forward_kernel, turn, width), grid_spec=...]
    psum x2 -> x0, blocking collectives: 64.8 us -> none  [the longest x1 40.7 us: local(): latent = lax.psum(latent_part, 'feat').astype(jnp.bfloat16)]
    reshape x9 -> x0, local copies, waits for them, and re-layouts: 62.2 us -> none  [the longest x1 14.3 us: local(): sparse.reshape(tok_rows, out_rows)]
    squeeze x1 -> x0, local copies, waits for them, and re-layouts: 39.3 us -> none  [local(): spread[:, :, level, :]]
    ppermute x4 -> x17, waiting for transfers between devices: 16 us -> 51.8 us  [from_partner(): return lax.ppermute(value, axis, pairs)]
    unnamed x29 -> x37, local copies, waits for them, and re-layouts: 31.8 us -> 3.31 us
  transfers between devices with their start and end apart: 8 -> 24, of which waited for: 2 -> 7; matrix products, arithmetic and copies ran while one was open for 60% -> 10% of each run, Pallas kernels for 0% -> 42%
where the time goes in v1:
time: 236 us; the launch traced here: 235 us
  Pallas kernels  103 us (44%)
  waiting for transfers between devices  51.8 us (22%)
  starting transfers between devices  45.4 us (19%)
  other arithmetic  21.9 us (9%)
  local copies, waits for them, and re-layouts  8.67 us (4%)
  matrix products  2.72 us (1%)
    pallas_call x4, Pallas kernels, forward_chunk(): pl.pallas_call(functools.partial(forward_kernel, turn, width), grid_spec=...  57.6 us
    ppermute x17, waiting for transfers between devices, from_partner(): return lax.ppermute(value, axis, pairs)  51.8 us
    pallas_call x3, Pallas kernels, spread(): pl.pallas_call(functools.partial(spread_kernel, turn, steps, width, tuple...  35.9 us
    ppermute x17, starting transfers between devices, from_partner(): return lax.ppermute(value, axis, pairs)  18.8 us
    ppermute x4, starting transfers between devices, line_hop(): return lax.ppermute(value, 'seq', pairs)  14.4 us
    all_to_all x3, starting transfers between devices, to_owner(): lax.all_to_all(value, 'feat', split_axis=0, concat_axis=0, tiled=True)  12.2 us
    pallas_call x1, Pallas kernels, merge_terms(): pl.pallas_call(functools.partial(merge_kernel, tuple(remote), tuple(dista...  5.72 us
  transfers between devices with their start and end apart: 24, of which 7 were waited for; matrix products, arithmetic and copies ran while one was open for 10% of the time, Pallas kernels for 42%

profile of v1, /device:TPU:0, one launch (start us, length us, event | category | flops | bytes accessed | tf_op | source)
XLA Modules:
  0.0 234.7 jit_solution(14356895176384891330)
XLA Ops:
  0.6 2.7 %fusion.13 = (bf16[512,256]{1,0:T(8,128)(2,1)S(1)}, f32[512,256]{1,0:T(8,128)S(1)}) fusion(bf16[512,2048]{1,0:T(8,128)(2,1)} %tokens_ref.1, bf16[2048,256]{1,0:T(8,128)(2,1)} %refs_1_.1), kind=kOutput, calls=%fused_computation.28 | convolution fusion | flops 537001984 | bytes 3932160 | tf_op jit(solution)/shard_map/dot_general | solution.py:290
  3.4 3.0 %collective-permute-start = (bf16[512,256]{1,0:T(8,128)(2,1)S(1)}, bf16[512,256]{1,0:T(8,128)(2,1)S(1)}, u32[]{:S(2)}, u32[]{:S(2)}) collective-permute-start(bf16[512,256]{1,0:T(8,128)(2,1)S(1)} %get-tuple-element.105), channel_id=1, source_target_pairs={{0,16},{8,24},{16,0},{24,8},{1,17},{9,25},{17,1},{25,9},{2,18},{10... | collective-permute-start | bytes 786440 | tf_op jit(solution)/shard_map/ppermute | solution.py:26
  9.0 3.7 %collective-permute-done = bf16[512,256]{1,0:T(8,128)(2,1)S(1)} collective-permute-done((bf16[512,256]{1,0:T(8,128)(2,1)S(1)}, bf16[512,256]{1,0:T(8,128)(2,1)S(1)}, u32[]{:S(2)}, u32[]{:S(2)}) %collective-permute-start) | collective-permute-done | bytes 262176 | tf_op jit(solution)/shard_map/ppermute | solution.py:26
  13.8 1.7 collective-permute-start.4
  19.5 19.9 %collective-permute-done.3 = bf16[512,256]{1,0:T(8,128)(2,1)S(1)} collective-permute-done((bf16[512,256]{1,0:T(8,128)(2,1)S(1)}, bf16[512,256]{1,0:T(8,128)(2,1)S(1)}, u32[]{:S(2)}, u32[]{:S(2)}) %collective-permute-start.3) | collective-permute-done | bytes 262176 | tf_op jit(solution)/shard_map/ppermute | solution.py:26
  40.2 14.4 %forward_chunk.4 = (bf16[512,7168]{1,0:T(8,128)(2,1)}, bf16[512,7168]{1,0:T(8,128)(2,1)}, bf16[1792,768]{1,0:T(8,128)(2,1)}, f32[512,256]{1,0:T(8,128)}) custom-call(s32[56,4]{1,0:T(8,128)} %copy.21.pattern_ref, s32[10]{0:T(128)} %stack.41.place_ref, bf16[512,2048]{1,0:T(8,128)(2,1)} %tokens_ref.1, bf16[512,1024]{1,0:T(8,128)(2,1)} %collective-permute-done.4.refs_1_, ...), custom_call_target="tpu_custom_call" | custom-call | flops 30000001024 | bytes 25165824 | tf_op jit(solution)/shard_map/forward_chunk/pallas_call | solution.py:106
  54.6 5.8 %collective-permute-done.2.refs_11_.refs_2_ = bf16[512,1024]{1,0:T(8,128)(2,1)S(1)} collective-permute-done((bf16[512,1024]{1,0:T(8,128)(2,1)S(1)}, bf16[512,1024]{1,0:T(8,128)(2,1)S(1)}, u32[]{:S(2)}, u32[]{:S(2)}) %collective-permute-start.2) | collective-permute-done | bytes 1048608 | tf_op jit(solution)/shard_map/ppermute | solution.py:26
  61.9 14.3 %forward_chunk.5 = (bf16[512,7168]{1,0:T(8,128)(2,1)}, bf16[512,7168]{1,0:T(8,128)(2,1)}, bf16[1792,768]{1,0:T(8,128)(2,1)}, f32[512,256]{1,0:T(8,128)}) custom-call(s32[56,4]{1,0:T(8,128)} %copy.21.pattern_ref, s32[10]{0:T(128)} %stack.41.place_ref, bf16[512,2048]{1,0:T(8,128)(2,1)} %tokens_ref.1, ...), custom_call_target="tpu_custom_call", output_to_operand_aliasing={{0}: (10, {}), {1}: (11, {})} | custom-call | flops 30000001024 | bytes 25165824 | tf_op jit(solution)/shard_map/forward_chunk/pallas_call | solution.py:106
  77.8 2.4 %fusion.3 = bf16[896,768]{1,0:T(8,128)(2,1)S(1)} fusion(bf16[1,2,896,768]{3,2,1,0:T(8,128)(2,1)} %bitcast.50, s32[]{:T(128)S(6)} %select_n.40, bf16[1,2,896,768]{3,2,1,0:T(8,128)(2,1)} %bitcast.49), kind=kLoop, calls=%fused_computation.9 | loop fusion | flops 2752512 | bytes 4128772 | tf_op jit(solution)/shard_map/convert_element_type | solution.py:353
  80.2 4.5 %collective-permute-start.8 = (bf16[896,768]{1,0:T(8,128)(2,1)S(1)}, bf16[896,768]{1,0:T(8,128)(2,1)}, u32[]{:S(2)}, u32[]{:S(2)}) collective-permute-start(bf16[896,768]{1,0:T(8,128)(2,1)S(1)} %fusion.3), channel_id=1, source_target_pairs={{0,2},{1,3},{6,4},{7,5},{8,10},{9,11},{14,12},{15,13},{16,18},{17,... | collective-permute-start | bytes 4128776 | tf_op jit(solution)/shard_map/ppermute | solution.py:341
  84.7 9.8 %spread.3 = bf16[512,2048]{1,0:T(8,128)(2,1)} custom-call(s32[56,4]{1,0:T(8,128)} %copy.21.pattern_ref, s32[10]{0:T(128)} %stack.41.place_ref, bf16[512,7168]{1,0:T(8,128)(2,1)} %get-tuple-element.64.grad_ref.refs_9_, bf16[7168,512]{1,0:T(8,128)(2,1)} %weight_ref.5), custom_call_target="tpu_custom_call" | custom-call | flops 30000001024 | bytes 25165824 | tf_op jit(solution)/shard_map/spread/pallas_call | solution.py:173
  94.5 3.8 %all-to-all-start = ((bf16[4,128,2048]{2,1,0:T(8,128)(2,1)}), bf16[4,128,2048]{2,1,0:T(8,128)(2,1)S(1)}, u32[]{:S(2)}, u32[]{:S(2)}) async-start(bf16[4,128,2048]{2,1,0:T(8,128)(2,1)} %bitcast.47), calls=%async_computation | async-start | bytes 4194304 | tf_op jit(solution)/shard_map/all_to_all | solution.py:317
  98.3 14.5 %forward_chunk.6 = (bf16[512,7168]{1,0:T(8,128)(2,1)}, bf16[512,7168]{1,0:T(8,128)(2,1)}, bf16[1792,768]{1,0:T(8,128)(2,1)}, f32[512,256]{1,0:T(8,128)}) custom-call(s32[56,4]{1,0:T(8,128)} %copy.21.pattern_ref, s32[10]{0:T(128)} %stack.41.place_ref, bf16[512,2048]{1,0:T(8,128)(2,1)} %tokens_ref.1, ...), custom_call_target="tpu_custom_call", output_to_operand_aliasing={{0}: (10, {}), {1}: (11, {})} | custom-call | flops 30000001024 | bytes 25165824 | tf_op jit(solution)/shard_map/forward_chunk/pallas_call | solution.py:106
  112.8 3.9 %add_convert_fusion.1 = (bf16[896,768]{1,0:T(8,128)(2,1)}, bf16[896,768]{1,0:T(8,128)(2,1)}) fusion(bf16[896,768]{1,0:T(8,128)(2,1)} %collective-permute-done.8, bf16[1,2,896,768]{3,2,1,0:T(8,128)(2,1)} %bitcast.14, s32[]{:T(128)S(6)} %select_n.40, bf16[1,2,896,768]{3,2,1,0:T(8,128)(2,1)S(1)} %bitcast.48), kind=kLoop, calls=%fused_computation.6 | loop fusion | flops 5505024 | bytes 6881284 | tf_op jit(solution)/shard_map/convert_element_type | solution.py:366
  118.4 6.3 %collective-permute-start.14 = (bf16[896,768]{1,0:T(8,128)(2,1)}, bf16[896,768]{1,0:T(8,128)(2,1)}, u32[]{:S(2)}, u32[]{:S(2)}) collective-permute-start(bf16[896,768]{1,0:T(8,128)(2,1)} %get-tuple-element.100), channel_id=1, source_target_pairs={{0,2},{1,3},{6,4},{7,5},{8,10},{9,11},{14,12},{15,13},{16,18},{17,... | collective-permute-start | bytes 4128776 | tf_op jit(solution)/shard_map/ppermute | solution.py:341
  124.7 14.4 %forward_chunk.7 = (bf16[512,7168]{1,0:T(8,128)(2,1)}, bf16[512,7168]{1,0:T(8,128)(2,1)}, bf16[1792,768]{1,0:T(8,128)(2,1)}, f32[512,256]{1,0:T(8,128)}) custom-call(s32[56,4]{1,0:T(8,128)} %copy.21.pattern_ref, s32[10]{0:T(128)} %stack.41.place_ref, bf16[512,2048]{1,0:T(8,128)(2,1)} %tokens_ref.1, ...), custom_call_target="tpu_custom_call", output_to_operand_aliasing={{0}: (10, {}), {1}: (11, {})} | custom-call | flops 30000001024 | bytes 25165824 | tf_op jit(solution)/shard_map/forward_chunk/pallas_call | solution.py:106
  139.1 3.2 %fusion.12 = (bf16[512,256]{1,0:T(8,128)(2,1)S(1)}, f32[512,256]{1,0:T(8,128)}) fusion(f32[512,256]{1,0:T(8,128)} %get-tuple-element.82, f32[512,256]{1,0:T(8,128)} %get-tuple-element.81, f32[512,256]{1,0:T(8,128)} %get-tuple-element.79, f32[512,256]{1,0:T(8,128)} %get-tuple-element.80), kind=kLoop, calls=%fused_computation.27 | loop fusion | flops 524288 | bytes 2883584 | tf_op jit(solution)/shard_map/convert_element_type | solution.py:373
  142.4 2.0 collective-permute-start.13
  145.9 9.8 %spread.4 = bf16[512,2048]{1,0:T(8,128)(2,1)} custom-call(s32[56,4]{1,0:T(8,128)} %copy.21.pattern_ref, s32[10]{0:T(128)} %stack.41.place_ref, bf16[512,7168]{1,0:T(8,128)(2,1)} %get-tuple-element.85.grad_ref, bf16[7168,512]{1,0:T(8,128)(2,1)} %weight_ref.5), custom_call_target="tpu_custom_call" | custom-call | flops 30000001024 | bytes 25165824 | tf_op jit(solution)/shard_map/spread/pallas_call | solution.py:173
  155.7 1.9 collective-permute-done.12
  157.6 2.9 %add_convert_fusion = bf16[896,768]{1,0:T(8,128)(2,1)} fusion(bf16[896,768]{1,0:T(8,128)(2,1)} %collective-permute-done.14, bf16[896,768]{1,0:T(8,128)(2,1)S(1)} %fusion.3), kind=kLoop, calls=%fused_computation.5 | loop fusion | flops 2752512 | bytes 4128768 | tf_op jit(solution)/shard_map/convert_element_type | solution.py:381
  160.6 4.0 %all-to-all-start.2 = ((bf16[4,128,2048]{2,1,0:T(8,128)(2,1)}), bf16[4,128,2048]{2,1,0:T(8,128)(2,1)S(1)}, u32[]{:S(2)}, u32[]{:S(2)}) async-start(bf16[4,128,2048]{2,1,0:T(8,128)(2,1)} %bitcast.46), calls=%async_computation.2 | async-start | bytes 4194304 | tf_op jit(solution)/shard_map/all_to_all | solution.py:317
  165.4 4.0 %right_sums.1 = (bf16[4,256,256]{2,1,0:T(8,128)(2,1)}, bf16[4,256,256]{2,1,0:T(8,128)(2,1)}) custom-call(s32[10]{0:T(128)} %stack.41.place_ref, bf16[512,2048]{1,0:T(8,128)(2,1)} %tokens_ref.1, bf16[512,256]{1,0:T(8,128)(2,1)} %add_convert_fusion.4.refs_0_.back_ref), custom_call_target="tpu_custom_call" | custom-call | tf_op jit(solution)/shard_map/right_sums/pallas_call | solution.py:239
  169.5 1.8 collective-permute-start.17
  171.3 2.7 %fusion = bf16[896,768]{1,0:T(8,128)(2,1)S(1)} fusion(bf16[896,768]{1,0:T(8,128)(2,1)} %collective-permute-done.15, bf16[1,2,896,768]{3,2,1,0:T(8,128)(2,1)} %bitcast.22, s32[]{:T(128)S(6)} %select_n.40, bf16[1,2,896,768]{3,2,1,0:T(8,128)(2,1)} %bitcast.21), kind=kLoop, calls=%fused_computation.1 | loop fusion | flops 4128768 | bytes 5505028 | tf_op jit(solution)/shard_map/convert_element_type | solution.py:382
  174.0 4.7 %collective-permute-start.18 = (bf16[896,768]{1,0:T(8,128)(2,1)S(1)}, bf16[896,768]{1,0:T(8,128)(2,1)}, u32[]{:S(2)}, u32[]{:S(2)}) collective-permute-start(bf16[896,768]{1,0:T(8,128)(2,1)S(1)} %fusion), channel_id=1, source_target_pairs={{0,2},{1,3},{2,0},{3,1},{4,6},{5,7},{6,4},{7,5},{8,10},{9,11},{10,... | collective-permute-start | bytes 4128776 | tf_op jit(solution)/shard_map/ppermute | solution.py:26
  178.7 16.3 %spread.5 = bf16[512,2048]{1,0:T(8,128)(2,1)} custom-call(s32[56,4]{1,0:T(8,128)} %copy.21.pattern_ref, s32[10]{0:T(128)} %stack.41.place_ref, bf16[512,7168]{1,0:T(8,128)(2,1)} %get-tuple-element.85.grad_ref, bf16[7168,512]{1,0:T(8,128)(2,1)} %weight_ref.5, bf16[512,256]{1,0:T(8,128)(2,1)} %add_convert_fusion.4.refs_0_.back_ref, bf16[2048,256]{1,0:T(8,128)(2,1)} %refs_1_.1), custom_call_target="tpu_custom_call" | custom-call | flops 30000001024 | bytes 25165824 | tf_op jit(solution)/shard_map/spread/pallas_call | solution.py:173
  195.0 4.4 %all-to-all-start.1 = ((bf16[4,128,2048]{2,1,0:T(8,128)(2,1)}), bf16[4,128,2048]{2,1,0:T(8,128)(2,1)}, u32[]{:S(2)}, u32[]{:S(2)}) async-start(bf16[4,128,2048]{2,1,0:T(8,128)(2,1)} %bitcast.45), calls=%async_computation.1 | async-start | bytes 4194304 | tf_op jit(solution)/shard_map/all_to_all | solution.py:317
  201.1 13.3 %collective-permute-done.19 = bf16[2,256,256]{2,1,0:T(8,128)(2,1)S(1)} collective-permute-done((bf16[2,256,256]{2,1,0:T(8,128)(2,1)S(1)}, bf16[2,256,256]{2,1,0:T(8,128)(2,1)S(1)}, u32[]{:S(2)}, u32[]{:S(2)}) %collective-permute-start.19) | collective-permute-done | bytes 262176 | tf_op jit(solution)/shard_map/ppermute | solution.py:26
  216.1 6.7 %collective-permute-done.20 = bf16[256,256]{1,0:T(8,128)(2,1)S(1)} collective-permute-done((bf16[256,256]{1,0:T(8,128)(2,1)S(1)}, bf16[256,256]{1,0:T(8,128)(2,1)S(1)}, u32[]{:S(2)}, u32[]{:S(2)}) %collective-permute-start.20) | collective-permute-done | bytes 131104 | tf_op jit(solution)/shard_map/ppermute | solution.py:26
  223.6 2.9 %fusion.2 = f32[896,768]{1,0:T(8,128)S(1)} fusion(bf16[896,768]{1,0:T(8,128)(2,1)} %collective-permute-done.18, bf16[896,768]{1,0:T(8,128)(2,1)} %collective-permute-done.17, bf16[1,2,896,768]{3,2,1,0:T(8,128)(2,1)} %bitcast.19, s32[]{:T(128)S(6)} %select_n.40, bf16[1,2,896,768]{3,2,1,0:T(8,128)(2,1)S(1)} %bitcast.51), kind=kLoop, calls=%fused_computation.4 | loop fusion | flops 5505024 | bytes 8257540 | tf_op jit(solution)/shard_map/mul | solution.py:399
  229.0 5.7 %merge_terms.1 = bf16[1,128,8192]{2,1,0:T(8,128)(2,1)} custom-call(s32[10]{0:T(128)} %stack.41.place_ref, bf16[4,128,2048]{2,1,0:T(8,128)(2,1)} %all-to-all-done.1.own_ref, bf16[4,128,2048]{2,1,0:T(8,128)(2,1)} %copy-done.1, bf16[4,128,2048]{2,1,0:T(8,128)(2,1)} %copy-done.2), custom_call_target="tpu_custom_call" | custom-call | tf_op jit(solution)/shard_map/merge_terms/pallas_call | solution.py:207
  (83 shorter events, 22.3 us)
Async XLA Ops:
  0.6 5.8 %copy-start = (bf16[512,2048]{1,0:T(8,128)(2,1)S(1)}, bf16[512,2048]{1,0:T(8,128)(2,1)}, u32[]{:S(2)}) copy-start(bf16[512,2048]{1,0:T(8,128)(2,1)} %tokens_ref.1) | copy-start | bytes 6291460
  3.4 9.3 %collective-permute-start = (bf16[512,256]{1,0:T(8,128)(2,1)S(1)}, bf16[512,256]{1,0:T(8,128)(2,1)S(1)}, u32[]{:S(2)}, u32[]{:S(2)}) collective-permute-start(bf16[512,256]{1,0:T(8,128)(2,1)S(1)} %get-tuple-element.105), channel_id=1, source_target_pairs={{0,16},{8,24},{16,0},{24,8},{1,17},{9,25},{17,1},{25,9},{2,18},{10... | collective-permute-start | bytes 786440 | tf_op jit(solution)/shard_map/ppermute | solution.py:26
  6.4 10.8 %copy-start.15 = (s32[56,4]{0,1:T(4,128)S(1)}, s32[56,4]{0,1:T(4,128)}, u32[]{:S(2)}) copy-start(s32[56,4]{0,1:T(4,128)} %param.10) | copy-start | bytes 2692
  7.5 32.7 %collective-permute-start.5 = (bf16[512,1024]{1,0:T(8,128)(2,1)}, bf16[512,1024]{1,0:T(8,128)(2,1)}, u32[]{:S(2)}, u32[]{:S(2)}) collective-permute-start(bf16[512,1024]{1,0:T(8,128)(2,1)} %constant_dynamic-slice_fusion), channel_id=1, source_target_pairs={{0,8},{8,0},{16,24},{24,16},{1,9},{9,1},{17,25},{25,17},{2,10},{10... | collective-permute-start | bytes 3145736 | tf_op jit(solution)/shard_map/ppermute | solution.py:26
  13.8 26.4 %collective-permute-start.4 = (bf16[512,1024]{1,0:T(8,128)(2,1)}, bf16[512,1024]{1,0:T(8,128)(2,1)}, u32[]{:S(2)}, u32[]{:S(2)}) collective-permute-start(bf16[512,1024]{1,0:T(8,128)(2,1)} %constant_dynamic-slice_fusion.1), channel_id=1, source_target_pairs={{0,16},{8,24},{16,0},{24,8},{1,17},{9,25},{17,1},{25,9},{2,18},{10... | collective-permute-start | bytes 3145736 | tf_op jit(solution)/shard_map/ppermute | solution.py:26
  15.6 23.8 %collective-permute-start.3 = (bf16[512,256]{1,0:T(8,128)(2,1)S(1)}, bf16[512,256]{1,0:T(8,128)(2,1)S(1)}, u32[]{:S(2)}, u32[]{:S(2)}) collective-permute-start(bf16[512,256]{1,0:T(8,128)(2,1)S(1)} %convert_element_type.154), channel_id=1, source_target_pairs={{0,8},{8,0},{16,24},{24,16},{1,9},{9,1},{17,25},{25,17},{2,10},{10... | collective-permute-start | bytes 786440 | tf_op jit(solution)/shard_map/ppermute | solution.py:26
  18.6 41.8 %collective-permute-start.2 = (bf16[512,1024]{1,0:T(8,128)(2,1)S(1)}, bf16[512,1024]{1,0:T(8,128)(2,1)S(1)}, u32[]{:S(2)}, u32[]{:S(2)}) collective-permute-start(bf16[512,1024]{1,0:T(8,128)(2,1)S(1)} %constant_dynamic-slice_fusion.2), channel_id=1, source_target_pairs={{0,8},{8,0},{16,24},{24,16},{1,9},{9,1},{17,25},{25,17},{2,10},{10... | collective-permute-start | bytes 3145736 | tf_op jit(solution)/shard_map/ppermute | solution.py:26
  19.2 41.7 %collective-permute-start.1 = (bf16[512,1024]{1,0:T(8,128)(2,1)S(1)}, bf16[512,1024]{1,0:T(8,128)(2,1)S(1)}, u32[]{:S(2)}, u32[]{:S(2)}) collective-permute-start(bf16[512,1024]{1,0:T(8,128)(2,1)S(1)} %constant_dynamic-slice_fusion.2), channel_id=1, source_target_pairs={{0,16},{8,24},{16,0},{24,8},{1,17},{9,25},{17,1},{25,9},{2,18},{10... | collective-permute-start | bytes 3145736 | tf_op jit(solution)/shard_map/ppermute | solution.py:26
  54.6 21.7 %collective-permute-start.6 = (bf16[1792,768]{1,0:T(8,128)(2,1)}, bf16[1792,768]{1,0:T(8,128)(2,1)S(1)}, u32[]{:S(2)}, u32[]{:S(2)}) collective-permute-start(bf16[1792,768]{1,0:T(8,128)(2,1)} %get-tuple-element.61), channel_id=1, source_target_pairs={{0,1},{1,0},{2,3},{3,2},{4,5},{5,4},{6,7},{7,6},{8,9},{9,8},{10,11... | collective-permute-start | bytes 8257544 | tf_op jit(solution)/shard_map/ppermute | solution.py:26
  76.3 8.4 %copy-start.4 = (bf16[1792,768]{1,0:T(8,128)(2,1)S(1)}, bf16[1792,768]{1,0:T(8,128)(2,1)}, u32[]{:S(2)}) copy-start(bf16[1792,768]{1,0:T(8,128)(2,1)} %get-tuple-element.63) | copy-start | bytes 8257540
  80.2 32.6 %collective-permute-start.8 = (bf16[896,768]{1,0:T(8,128)(2,1)S(1)}, bf16[896,768]{1,0:T(8,128)(2,1)}, u32[]{:S(2)}, u32[]{:S(2)}) collective-permute-start(bf16[896,768]{1,0:T(8,128)(2,1)S(1)} %fusion.3), channel_id=1, source_target_pairs={{0,2},{1,3},{6,4},{7,5},{8,10},{9,11},{14,12},{15,13},{16,18},{17,... | collective-permute-start | bytes 4128776 | tf_op jit(solution)/shard_map/ppermute | solution.py:341
  84.7 9.8 %collective-permute-start.7 = (bf16[1792,768]{1,0:T(8,128)(2,1)S(1)}, bf16[1792,768]{1,0:T(8,128)(2,1)}, u32[]{:S(2)}, u32[]{:S(2)}) collective-permute-start(bf16[1792,768]{1,0:T(8,128)(2,1)S(1)} %copy-done.4), channel_id=1, source_target_pairs={{0,1},{1,0},{2,3},{3,2},{4,5},{5,4},{6,7},{7,6},{8,9},{9,8},{10,11... | collective-permute-start | bytes 8257544 | tf_op jit(solution)/shard_map/ppermute | solution.py:26
  94.5 44.6 %all-to-all-start = ((bf16[4,128,2048]{2,1,0:T(8,128)(2,1)}), bf16[4,128,2048]{2,1,0:T(8,128)(2,1)S(1)}, u32[]{:S(2)}, u32[]{:S(2)}) async-start(bf16[4,128,2048]{2,1,0:T(8,128)(2,1)} %bitcast.47), calls=%async_computation | async-start | bytes 4194304 | tf_op jit(solution)/shard_map/all_to_all | solution.py:317
  98.3 14.5 %copy-start.5 = (bf16[1792,768]{1,0:T(8,128)(2,1)S(1)}, bf16[1792,768]{1,0:T(8,128)(2,1)}, u32[]{:S(2)}) copy-start(bf16[1792,768]{1,0:T(8,128)(2,1)} %get-tuple-element.63) | copy-start | bytes 8257540
  116.7 29.2 %collective-permute-start.15 = (bf16[896,768]{1,0:T(8,128)(2,1)}, bf16[896,768]{1,0:T(8,128)(2,1)}, u32[]{:S(2)}, u32[]{:S(2)}) collective-permute-start(bf16[896,768]{1,0:T(8,128)(2,1)} %get-tuple-element.99), channel_id=1, source_target_pairs={{2,4},{3,5},{4,2},{5,3},{10,12},{11,13},{12,10},{13,11},{18,20},{1... | collective-permute-start | bytes 4128776 | tf_op jit(solution)/shard_map/ppermute | solution.py:341
  118.4 37.3 %collective-permute-start.14 = (bf16[896,768]{1,0:T(8,128)(2,1)}, bf16[896,768]{1,0:T(8,128)(2,1)}, u32[]{:S(2)}, u32[]{:S(2)}) collective-permute-start(bf16[896,768]{1,0:T(8,128)(2,1)} %get-tuple-element.100), channel_id=1, source_target_pairs={{0,2},{1,3},{6,4},{7,5},{8,10},{9,11},{14,12},{15,13},{16,18},{17,... | collective-permute-start | bytes 4128776 | tf_op jit(solution)/shard_map/ppermute | solution.py:341
  124.7 14.4 %collective-permute-start.9 = (bf16[1792,768]{1,0:T(8,128)(2,1)}, bf16[1792,768]{1,0:T(8,128)(2,1)}, u32[]{:S(2)}, u32[]{:S(2)}) collective-permute-start(bf16[1792,768]{1,0:T(8,128)(2,1)} %get-tuple-element.75), channel_id=1, source_target_pairs={{0,1},{1,0},{2,3},{3,2},{4,5},{5,4},{6,7},{7,6},{8,9},{9,8},{10,11... | collective-permute-start | bytes 8257544 | tf_op jit(solution)/shard_map/ppermute | solution.py:26
  139.1 16.6 %copy-start.1 = (bf16[4,128,2048]{2,1,0:T(8,128)(2,1)}, bf16[4,128,2048]{2,1,0:T(8,128)(2,1)S(1)}, u32[]{:S(2)}) copy-start(bf16[4,128,2048]{2,1,0:T(8,128)(2,1)S(1)} %all-to-all-done.refs_0_) | copy-start | bytes 6291460
  139.1 6.8 %copy-start.7 = (bf16[1792,768]{1,0:T(8,128)(2,1)S(1)}, bf16[1792,768]{1,0:T(8,128)(2,1)}, u32[]{:S(2)}) copy-start(bf16[1792,768]{1,0:T(8,128)(2,1)} %get-tuple-element.78) | copy-start | bytes 8257540
  142.4 13.4 %collective-permute-start.13 = (bf16[512,256]{1,0:T(8,128)(2,1)S(1)}, bf16[512,256]{1,0:T(8,128)(2,1)S(1)}, u32[]{:S(2)}, u32[]{:S(2)}) collective-permute-start(bf16[512,256]{1,0:T(8,128)(2,1)S(1)} %get-tuple-element.101), channel_id=1, source_target_pairs={{0,24},{8,16},{16,8},{24,0},{1,25},{9,17},{17,9},{25,1},{2,26},{10... | collective-permute-start | bytes 786440 | tf_op jit(solution)/shard_map/ppermute | solution.py:26
  144.3 13.2 %collective-permute-start.12 = (bf16[512,256]{1,0:T(8,128)(2,1)S(1)}, bf16[512,256]{1,0:T(8,128)(2,1)S(1)}, u32[]{:S(2)}, u32[]{:S(2)}) collective-permute-start(bf16[512,256]{1,0:T(8,128)(2,1)S(1)} %get-tuple-element.101), channel_id=1, source_target_pairs={{0,16},{8,24},{16,0},{24,8},{1,17},{9,25},{17,1},{25,9},{2,18},{10... | collective-permute-start | bytes 786440 | tf_op jit(solution)/shard_map/ppermute | solution.py:26
  145.3 12.3 %collective-permute-start.11 = (bf16[512,256]{1,0:T(8,128)(2,1)S(1)}, bf16[512,256]{1,0:T(8,128)(2,1)S(1)}, u32[]{:S(2)}, u32[]{:S(2)}) collective-permute-start(bf16[512,256]{1,0:T(8,128)(2,1)S(1)} %get-tuple-element.101), channel_id=1, source_target_pairs={{0,8},{8,0},{16,24},{24,16},{1,9},{9,1},{17,25},{25,17},{2,10},{10... | collective-permute-start | bytes 786440 | tf_op jit(solution)/shard_map/ppermute | solution.py:26
  145.9 11.7 %collective-permute-start.10 = (bf16[1792,768]{1,0:T(8,128)(2,1)S(1)}, bf16[1792,768]{1,0:T(8,128)(2,1)}, u32[]{:S(2)}, u32[]{:S(2)}) collective-permute-start(bf16[1792,768]{1,0:T(8,128)(2,1)S(1)} %copy-done.7), channel_id=1, source_target_pairs={{0,1},{1,0},{2,3},{3,2},{4,5},{5,4},{6,7},{7,6},{8,9},{9,8},{10,11... | collective-permute-start | bytes 8257544 | tf_op jit(solution)/shard_map/ppermute | solution.py:26
  160.6 34.4 %all-to-all-start.2 = ((bf16[4,128,2048]{2,1,0:T(8,128)(2,1)}), bf16[4,128,2048]{2,1,0:T(8,128)(2,1)S(1)}, u32[]{:S(2)}, u32[]{:S(2)}) async-start(bf16[4,128,2048]{2,1,0:T(8,128)(2,1)} %bitcast.46), calls=%async_computation.2 | async-start | bytes 4194304 | tf_op jit(solution)/shard_map/all_to_all | solution.py:317
  169.5 25.5 %collective-permute-start.16 = (bf16[4,256,256]{2,1,0:T(8,128)(2,1)}, bf16[4,256,256]{2,1,0:T(8,128)(2,1)}, u32[]{:S(2)}, u32[]{:S(2)}) collective-permute-start(bf16[4,256,256]{2,1,0:T(8,128)(2,1)} %get-tuple-element.89), channel_id=1, source_target_pairs={{0,1},{1,0},{2,3},{3,2},{4,5},{5,4},{6,7},{7,6},{8,9},{9,8},{10,11... | collective-permute-start | bytes 1572872 | tf_op jit(solution)/shard_map/ppermute | solution.py:26
  169.5 54.1 %collective-permute-start.17 = (bf16[896,768]{1,0:T(8,128)(2,1)}, bf16[896,768]{1,0:T(8,128)(2,1)}, u32[]{:S(2)}, u32[]{:S(2)}) collective-permute-start(bf16[896,768]{1,0:T(8,128)(2,1)} %add_convert_fusion), channel_id=1, source_target_pairs={{2,4},{3,5},{4,2},{5,3},{10,12},{11,13},{12,10},{13,11},{18,20},{1... | collective-permute-start | bytes 4128776 | tf_op jit(solution)/shard_map/ppermute | solution.py:341
  174.0 49.6 %collective-permute-start.18 = (bf16[896,768]{1,0:T(8,128)(2,1)S(1)}, bf16[896,768]{1,0:T(8,128)(2,1)}, u32[]{:S(2)}, u32[]{:S(2)}) collective-permute-start(bf16[896,768]{1,0:T(8,128)(2,1)S(1)} %fusion), channel_id=1, source_target_pairs={{0,2},{1,3},{2,0},{3,1},{4,6},{5,7},{6,4},{7,5},{8,10},{9,11},{10,... | collective-permute-start | bytes 4128776 | tf_op jit(solution)/shard_map/ppermute | solution.py:26
  195.0 6.0 %copy-start.2 = (bf16[4,128,2048]{2,1,0:T(8,128)(2,1)}, bf16[4,128,2048]{2,1,0:T(8,128)(2,1)S(1)}, u32[]{:S(2)}) copy-start(bf16[4,128,2048]{2,1,0:T(8,128)(2,1)S(1)} %all-to-all-done.2.refs_1_) | copy-start | bytes 6291460
  195.0 34.0 %all-to-all-start.1 = ((bf16[4,128,2048]{2,1,0:T(8,128)(2,1)}), bf16[4,128,2048]{2,1,0:T(8,128)(2,1)}, u32[]{:S(2)}, u32[]{:S(2)}) async-start(bf16[4,128,2048]{2,1,0:T(8,128)(2,1)} %bitcast.45), calls=%async_computation.1 | async-start | bytes 4194304 | tf_op jit(solution)/shard_map/all_to_all | solution.py:317
  199.5 24.1 %copy-start.8 = (bf16[1792,768]{1,0:T(8,128)(2,1)S(1)}, bf16[1792,768]{1,0:T(8,128)(2,1)}, u32[]{:S(2)}) copy-start(bf16[1792,768]{1,0:T(8,128)(2,1)} %get-tuple-element.78) | copy-start | bytes 8257540
  201.0 13.4 %collective-permute-start.19 = (bf16[2,256,256]{2,1,0:T(8,128)(2,1)S(1)}, bf16[2,256,256]{2,1,0:T(8,128)(2,1)S(1)}, u32[]{:S(2)}, u32[]{:S(2)}) collective-permute-start(bf16[2,256,256]{2,1,0:T(8,128)(2,1)S(1)} %slice.19), channel_id=1, source_target_pairs={{0,2},{1,3},{2,0},{3,1},{4,6},{5,7},{6,4},{7,5},{8,10},{9,11},{10,... | collective-permute-start | bytes 786440 | tf_op jit(solution)/shard_map/ppermute | solution.py:26
  214.4 8.4 %collective-permute-start.20 = (bf16[256,256]{1,0:T(8,128)(2,1)S(1)}, bf16[256,256]{1,0:T(8,128)(2,1)S(1)}, u32[]{:S(2)}, u32[]{:S(2)}) collective-permute-start(bf16[256,256]{1,0:T(8,128)(2,1)S(1)} %fusion.9), channel_id=1, source_target_pairs={{0,4},{1,5},{2,6},{3,7},{4,0},{5,1},{6,2},{7,3},{8,12},{9,13},{10,... | collective-permute-start | bytes 393224 | tf_op jit(solution)/shard_map/ppermute | solution.py:26
  (10 other events, 30.4 us)

commit v2 on v1

--- a/solution.py
+++ b/solution.py
@@ -37,18 +37,19 @@
     step = pl.program_id(0)
     first = chunk_step(place_ref, turn, step) * STEP
 
-    def operands(row):
+    def picked(row):
         column = lax.rem(pattern_ref[first + row, 0], width)
         lanes = pl.ds(pl.multiple_of(column * BLK, BLK), BLK)
-        return jnp.concatenate([slab[:, lanes] for slab in slabs] + [latent_ref[...]], axis=1)
-
+        return jnp.concatenate([slab[:, lanes] for slab in slabs], axis=1)
+
+    across = (((1,), (1,)), ((), ()))
+    along = (((0,), (0,)), ((), ()))
     every = [slice(row * BLK, (row + 1) * BLK) for row in range(STEP)]
+    low = lax.dot_general(latent_ref[...], left_ref[...], across, preferred_element_type=F32)
     pres = []
     for row, rows in enumerate(every):
-        weights = jnp.concatenate([weight_ref[rows, :], left_ref[rows, :]], axis=1)
-        pres.append(
-            lax.dot_general(operands(row), weights, (((1,), (1,)), ((), ())), preferred_element_type=F32)
-        )
+        sparse = lax.dot_general(picked(row), weight_ref[rows, :], across, preferred_element_type=F32)
+        pres.append(sparse + low[:, rows])
     grads = []
     for pre, rows in zip(pres, every):
         square = pre * pre
@@ -59,11 +60,16 @@
         grad = (cot_ref[:, rows].astype(F32) * slope).astype(BF16)
         grad_ref[:, rows] = grad
         grads.append(grad)
+    sparse_cols = LEVELS * BLK
     for row, rows in enumerate(every):
-        sums_ref[rows, :] = lax.dot_general(
-            grads[row], operands(row), (((0,), (0,)), ((), ())), preferred_element_type=F32
+        sums_ref[rows, :sparse_cols] = lax.dot_general(
+            grads[row], picked(row), along, preferred_element_type=F32
         ).astype(BF16)
-    back = jnp.dot(jnp.concatenate(grads, axis=1), left_ref[...], preferred_element_type=F32)
+    grads = jnp.concatenate(grads, axis=1)
+    sums_ref[:, sparse_cols:] = lax.dot_general(
+        grads, latent_ref[...], along, preferred_element_type=F32
+    ).astype(BF16)
+    back = jnp.dot(grads, left_ref[...], preferred_element_type=F32)
 
     @pl.when(step == 0)
     def _():
@@ -141,17 +147,14 @@
 
     weights = weight_ref[...]
     weights = jnp.concatenate([weights[:, level * BLK : (level + 1) * BLK] for level in levels], axis=1)
+    every = [slice(row * BLK, (row + 1) * BLK) for row in range(STEP)]
+    terms = [jnp.dot(grad_ref[:, cols], weights[cols, :], preferred_element_type=F32) for cols in every]
     for row in range(STEP):
-        cols = slice(row * BLK, (row + 1) * BLK)
         column = lax.rem(pattern_ref[first + row, 0], width)
-        terms = jnp.dot(grad_ref[:, cols], weights[cols, :], preferred_element_type=F32)
         for at, level in enumerate(levels):
-            if last:
-                begin = step_group(place_ref, turn, step) ^ moves[level]
-            else:
-                begin = at
+            begin = step_group(place_ref, turn, step) ^ moves[level] if last else at
             lanes = pl.ds(pl.multiple_of(begin * span + column * BLK, BLK), BLK)
-            total[:, lanes] += terms[:, at * BLK : (at + 1) * BLK]
+            total[:, lanes] += terms[row][:, at * BLK : (at + 1) * BLK]
 
     @pl.when(step == steps - 1)
     def _():
@@ -218,26 +221,19 @@
     )(place, own, *arrived)
 
 
-def right_kernel(bits, rows, place_ref, tokens_ref, back_ref, keep_ref, send_ref):
-    even = place_ref[1 + 2 * CHUNKS] == 0
+def right_kernel(place_ref, tokens_ref, back_ref, *outs):
+    cols = outs[0].shape[1]
     for turn in range(CHUNKS):
-        for pair in range(1 << (bits - 1)):
-            begin = ((place_ref[1 + turn] << (bits - 1)) + pair) * 2 * rows
-            lanes = pl.ds(pl.multiple_of(begin, 2 * rows), 2 * rows)
-            both = lax.dot_general(
-                tokens_ref[:, lanes], back_ref[...], (((0,), (0,)), ((), ())), preferred_element_type=F32
-            )
-            low, high = both[:rows], both[rows:]
-            at = slice(pair * rows, (pair + 1) * rows)
-            keep_ref[turn, at, :] = jnp.where(even, low, high).astype(BF16)
-            send_ref[turn, at, :] = jnp.where(even, high, low).astype(BF16)
-
-
-def right_sums(bits, count, place, tokens, back):
-    rows = tokens.shape[1] // count
-    shape = jax.ShapeDtypeStruct((CHUNKS, rows << (bits - 1), back.shape[1]), BF16)
+        lanes = pl.ds(pl.multiple_of(place_ref[1 + turn] * cols, cols), cols)
+        outs[turn % 2][turn // 2] = lax.dot_general(
+            tokens_ref[:, lanes], back_ref[...], (((0,), (0,)), ((), ())), preferred_element_type=F32
+        ).astype(BF16)
+
+
+def right_sums(place, tokens, back):
+    shape = jax.ShapeDtypeStruct((CHUNKS // 2, tokens.shape[1] // CHUNKS, back.shape[1]), BF16)
     return pl.pallas_call(
-        functools.partial(right_kernel, bits, rows),
+        right_kernel,
         grid_spec=pltpu.PrefetchScalarGridSpec(
             num_scalar_prefetch=1,
             grid=(1,),
@@ -250,16 +246,60 @@
     )(place, tokens, back)
 
 
-def pair_sums(value, other, index, bits):
+def pair_kernel(place_ref, *refs):
+    for mine, other, out in zip(refs[:2], refs[2:4], refs[4:]):
+        out[...] = (mine[...].astype(F32) + other[...].astype(F32)).astype(out.dtype)
+
+
+def pair_sums(place, total, swapped, index, bits, dtypes):
     count = 1 << bits
-    rows = value.shape[0] // count
-    split = lambda v: v.reshape(count // 2, 2, rows, v.shape[1])
-    mine = lambda v: lax.dynamic_index_in_dim(split(v), index & 1, 1, keepdims=False).astype(F32)
-    return lower_sums(mine(value) + mine(other), index, bits)
-
-
-def lower_sums(part, index, bits):
-    for bit in range(1, bits):
+    rows = total.shape[0] // 2 // count
+    cols = total.shape[1]
+    block = (rows // 2, cols)
+    specs = [
+        pl.BlockSpec(block, lambda i, h, w, turn=turn: ((turn * count + 2 * i + w[1 + 2 * CHUNKS]) * 2 + h, 0))
+        for turn in (0, 1)
+    ]
+    sums = pl.pallas_call(
+        pair_kernel,
+        grid_spec=pltpu.PrefetchScalarGridSpec(
+            num_scalar_prefetch=1,
+            grid=(count // 2, 2),
+            in_specs=specs * 2,
+            out_specs=[pl.BlockSpec(block, lambda i, h, w: (2 * i + h, 0))] * 2,
+        ),
+        out_shape=[jax.ShapeDtypeStruct((rows * count // 2, cols), dtype) for dtype in dtypes],
+        name="pair_sums",
+    )(place, total, total, swapped, swapped)
+    if bits == 1:
+        return sums
+    return [lower_sums(part.astype(F32).reshape(count // 2, rows, cols), index, 1, bits).astype(part.dtype) for part in sums]
+
+
+def final_kernel(scale, kept_ref, first_ref, second_ref, blocks_ref, left_ref):
+    total = kept_ref[...] + first_ref[...].astype(F32) + second_ref[...].astype(F32)
+    total = total * scale
+    cols = blocks_ref.shape[1]
+    blocks_ref[...] = total[:, :cols]
+    left_ref[...] = total[:, cols:]
+
+
+def final_sums(kept, first, second, scale):
+    rows, cols = kept.shape
+    split = LEVELS * BLK
+    block = lambda width: pl.BlockSpec((rows // 2, width), lambda h: (h, 0))
+    return pl.pallas_call(
+        functools.partial(final_kernel, scale),
+        grid=(2,),
+        in_specs=[block(cols)] * 3,
+        out_specs=[block(split), block(cols - split)],
+        out_shape=[jax.ShapeDtypeStruct((rows, width), F32) for width in (split, cols - split)],
+        name="final_sums",
+    )(kept, first, second)
+
+
+def lower_sums(part, index, first, bits):
+    for bit in range(first, bits):
         mine = (index >> bit) & 1
         part = part.reshape(part.shape[0] // 2, 2, *part.shape[1:])
         keep = lax.dynamic_index_in_dim(part, mine, 1, keepdims=False)
@@ -290,19 +330,21 @@
     latent_part = jnp.dot(tokens, right_factor, preferred_element_type=F32)
     distance = feat_count // 2
     other = from_partner(latent_part.astype(BF16), "feat", distance)
-    tokens_after, other = lax.optimization_barrier((tokens, other))
     received = []
     for turn in range(groups):
         group = (quarter ^ (CHUNKS - 1)) * groups // CHUNKS ^ turn
         piece = lax.dynamic_slice_in_dim(tokens, group * span, span, 1)
-        late = lax.dynamic_slice_in_dim(tokens_after, group * span, span, 1)
-        sources = [late if turn > 0 or d == feat_count // 2 else piece for d in distances]
+        if turn == 0:
+            late, other = lax.optimization_barrier((piece, other))
+        else:
+            piece, latent_part = lax.optimization_barrier((piece, latent_part))
+            late = piece
+        sources = [late if d == feat_count // 2 else piece for d in distances]
         received.append([from_partner(s, "feat", d) if d > 0 else None for s, d in zip(sources, distances)])
         if turn == 0:
             latent_part = latent_part + other.astype(F32)
             while distance > 1:
                 distance //= 2
-                tokens_after, latent_part = lax.optimization_barrier((tokens_after, latent_part))
                 latent_part = latent_part + from_partner(latent_part.astype(BF16), "feat", distance).astype(F32)
     latent = latent_part.astype(BF16)
 
@@ -345,61 +387,53 @@
     core_hop = lambda value: from_partner(value, "seq", 1)
     wide = lambda value: value.astype(F32)
 
-    act, grad, total0, back0 = forward(0, 1, None)
-    swap0 = core_hop(total0)
-    act, grad, total1, back1 = forward(1, 1, (act, grad), [slab for slab in received[-1] if slab is not None])
-    grad, total1, swap0 = hold((grad, total1, swap0))
-
-    sum0 = pair_sums(total0, swap0, index, bits).astype(BF16)
-    got0 = inward(sum0)
-    swap1 = core_hop(total1)
+    act, grad, total, back = forward(0, 2, None)
+    if groups > 1:
+        received[1], total, grad = hold((received[1], total, grad))
+    swapped = core_hop(total)
     arrived = []
     if groups > 1:
         terms = spread_levels(0, turns, grad, remote, (), len(remote) * span)
-        terms, swap1, grad = hold((terms, swap1, grad))
+        terms, swapped, grad = hold((terms, swapped, grad))
+    sum0, sum1 = pair_sums(place, total, swapped, index, bits, (BF16, BF16))
+    got0, got1 = inward(sum0), inward(sum1)
+    if groups > 1:
         arrived.append(to_owner(terms))
-    sum1 = pair_sums(total1, swap1, index, bits).astype(BF16)
-    got1 = inward(sum1)
-    act, grad, total2, back2 = forward(2, 1, (act, grad))
-    grad, total2, back2, got0 = hold((grad, total2, back2, got0))
+    act, grad, total, more = forward(2, 2, (act, grad))
+    grad, total, more, got0, arrived = hold((grad, total, more, got0, arrived))
 
     got2 = across((wide(sum1) + wide(got0)).astype(BF16))
-    swap2 = core_hop(total2)
-    act, grad, total3, back3 = forward(3, 1, (act, grad))
-    grad, total3, back3, swap2, arrived = hold((grad, total3, back3, swap2, arrived))
-
-    swap3 = core_hop(total3)
-    back = back0 + back1 + back2 + back3
+    back = back + more
     parts = others(back.astype(BF16), "feat")
-    sum2 = pair_sums(total2, swap2, index, bits)
+    swapped = core_hop(total)
     terms = spread_levels(CHUNKS - turns, turns, grad, remote, (), len(remote) * span)
-    terms, swap3, parts, got1, got2, grad = hold((terms, swap3, parts, got1, got2, grad))
+    terms, swapped, parts, grad = hold((terms, swapped, parts, grad))
 
     for part in parts:
         back = back + wide(part)
     back_latent = back.astype(BF16)
-    got3 = across((wide(sum0) + wide(got1)).astype(BF16))
-    got4 = near_hop((sum2 + wide(got2)).astype(BF16))
+    right_send, right_keep = right_sums(place, tokens, back_latent)
+    close = near_hop(right_send)
     arrived.append(to_owner(terms))
-    right_keep, right_send = right_sums(bits, seq_count, place, tokens, back_latent)
-    right_swap = core_hop(right_send)
+    sum2, sum3 = pair_sums(place, total, swapped, index, bits, (BF16, F32))
     own_levels = [level for level in range(LEVELS) if level not in remote]
-    own = spread_levels(0, CHUNKS, grad, own_levels, (back_latent, right_factor), local_width)
-    own, right_swap = hold((own, right_swap))
-
+    own = spread_levels(0, CHUNKS, grad, own_levels, (back_latent, right_factor), local_width, (sum3,))
+    own, close, got1, got2 = hold((own, close, got1, got2))
+
+    last_part = far_hop((wide(right_keep[0]) + wide(close[0])).astype(BF16))
     own = to_owner(own)
-    right = wide(right_keep) + wide(right_swap)
-    right = jnp.stack(
-        [lower_sums(part.reshape(1 << (bits - 1), -1, part.shape[1]), index, bits) for part in right]
-    )
-    close = near_hop(right[0::2].astype(BF16))
-    grad_right = right[3] + wide(close[1]) + wide(far_hop((right[1] + wide(close[0])).astype(BF16)))
-    grad_right = grad_right * norm_scale
-    final = pair_sums(total3, swap3, index, bits) + wide(got3) + wide(got4)
-    final = final * norm_scale
+    send4 = (wide(sum2) + wide(got2)).astype(BF16)
+    send3 = (wide(sum0) + wide(got1)).astype(BF16)
+    send4, send3, last_part = hold((send4, send3, last_part))
+    got4 = near_hop(send4)
+    got3 = across(send3)
+    right = wide(right_keep[1]) + wide(close[1]) + wide(last_part)
+    grad_right = lower_sums(right.reshape(1 << bits, -1, right.shape[1]), index, 0, bits) * norm_scale
     grad_input = merge_terms(place, own, arrived, remote, distances, span)
-
-    return (act, grad_input, final[:, : LEVELS * BLK], final[:, LEVELS * BLK :], grad_right)
+    grad_input, grad_right, got3, got4 = hold((grad_input, grad_right, got3, got4))
+    grad_blocks, grad_left = final_sums(sum3, got3, got4, norm_scale)
+
+    return (act, grad_input, grad_blocks, grad_left, grad_right)
 
 
 def solution(mesh):

time: 236 us -> 226 us (0.958)
  other arithmetic: 21.9 us -> 12.9 us
  local copies, waits for them, and re-layouts: 8.67 us -> 5.36 us
  waiting for transfers between devices: 51.8 us -> 54.3 us
    ppermute x17 -> x15, waiting for transfers between devices: 51.8 us -> 34.6 us  [from_partner(): return lax.ppermute(value, axis, pairs)]
    all_to_all x3, waiting for transfers between devices: 0.01 us -> 15.6 us  [to_owner(): lax.all_to_all(value, 'feat', split_axis=0, concat_axis=0, tiled=True)]
    pallas_call x1 -> x4, Pallas kernels: 4.04 us -> 17.2 us  [the longest x2 9.39 us: pair_sums(): pl.pallas_call(pair_kernel, grid_spec=pltpu.PrefetchScalarGridSpec(num_sc...]
    pallas_call x4 -> x2, Pallas kernels: 57.6 us -> 45.3 us  [forward_chunk(): pl.pallas_call(functools.partial(forward_kernel, turn, width), grid_spec=...]
    ppermute x4, waiting for transfers between devices: 0.01 us -> 4.06 us  [line_hop(): return lax.ppermute(value, 'seq', pairs)]
    convert_element_type x5 -> x2, other arithmetic: 8.75 us -> 5.27 us  [the longest x1 4.41 us: local(): send3 = (wide(sum0) + wide(got1)).astype(BF16)]
    mul x2 -> x1, other arithmetic: 3.64 us -> 0.73 us  [local(): lower_sums(right.reshape(1 << bits, -1, right.shape[1]), index, 0, bits)]
    ppermute x4, starting transfers between devices: 14.4 us -> 11.5 us  [line_hop(): return lax.ppermute(value, 'seq', pairs)]
  transfers between devices with their start and end apart: 24 -> 22, of which waited for: 7 -> 7; matrix products, arithmetic and copies ran while one was open for 10% -> 7% of each run, Pallas kernels for 42% -> 43%
where the time goes in v2:
time: 226 us; the launch traced here: 225 us
  Pallas kernels  104 us (46%)
  waiting for transfers between devices  54.3 us (24%)
  starting transfers between devices  44.3 us (20%)
  other arithmetic  12.9 us (6%)
  local copies, waits for them, and re-layouts  5.36 us (2%)
  matrix products  2.71 us (1%)
    pallas_call x2, Pallas kernels, forward_chunk(): pl.pallas_call(functools.partial(forward_kernel, turn, width), grid_spec=...  45.3 us
    pallas_call x3, Pallas kernels, spread(): pl.pallas_call(functools.partial(spread_kernel, turn, steps, width, tuple...  36.1 us
    ppermute x15, waiting for transfers between devices, from_partner(): return lax.ppermute(value, axis, pairs)  34.6 us
    ppermute x15, starting transfers between devices, from_partner(): return lax.ppermute(value, axis, pairs)  21.1 us
    all_to_all x3, waiting for transfers between devices, to_owner(): lax.all_to_all(value, 'feat', split_axis=0, concat_axis=0, tiled=True)  15.6 us
    all_to_all x3, starting transfers between devices, to_owner(): lax.all_to_all(value, 'feat', split_axis=0, concat_axis=0, tiled=True)  11.7 us
    ppermute x4, starting transfers between devices, line_hop(): return lax.ppermute(value, 'seq', pairs)  11.5 us
    pallas_call x2, Pallas kernels, pair_sums(): pl.pallas_call(pair_kernel, grid_spec=pltpu.PrefetchScalarGridSpec(num_sc...  9.39 us
  transfers between devices with their start and end apart: 22, of which 7 were waited for; matrix products, arithmetic and copies ran while one was open for 7% of the time, Pallas kernels for 43%

profile of v2, /device:TPU:0, one launch (start us, length us, event | category | flops | bytes accessed | tf_op | source)
XLA Modules:
  0.0 224.6 jit_solution(11960871337581922165)
XLA Ops:
  0.6 2.7 %fusion.6 = (bf16[512,256]{1,0:T(8,128)(2,1)S(1)}, f32[512,256]{1,0:T(8,128)S(1)}) fusion(bf16[512,2048]{1,0:T(8,128)(2,1)} %tokens_ref.1, bf16[2048,256]{1,0:T(8,128)(2,1)} %refs_1_.1), kind=kOutput, calls=%fused_computation.18 | convolution fusion | flops 537001984 | bytes 3932160 | tf_op jit(solution)/shard_map/dot_general | solution.py:330
  3.4 3.0 %collective-permute-start = (bf16[512,256]{1,0:T(8,128)(2,1)S(1)}, bf16[512,256]{1,0:T(8,128)(2,1)S(1)}, u32[]{:S(2)}, u32[]{:S(2)}) collective-permute-start(bf16[512,256]{1,0:T(8,128)(2,1)S(1)} %get-tuple-element.107), channel_id=1, source_target_pairs={{0,16},{8,24},{16,0},{24,8},{1,17},{9,25},{17,1},{25,9},{2,18},{10... | collective-permute-start | bytes 786440 | tf_op jit(solution)/shard_map/ppermute | solution.py:26
  9.4 3.3 %collective-permute-done = bf16[512,256]{1,0:T(8,128)(2,1)S(1)} collective-permute-done((bf16[512,256]{1,0:T(8,128)(2,1)S(1)}, bf16[512,256]{1,0:T(8,128)(2,1)S(1)}, u32[]{:S(2)}, u32[]{:S(2)}) %collective-permute-start) | collective-permute-done | bytes 262176 | tf_op jit(solution)/shard_map/ppermute | solution.py:26
  12.7 1.7 collective-permute-start.4
  14.5 1.6 collective-permute-start.1
  17.4 21.0 %collective-permute-done.1 = bf16[512,256]{1,0:T(8,128)(2,1)S(1)} collective-permute-done((bf16[512,256]{1,0:T(8,128)(2,1)S(1)}, bf16[512,256]{1,0:T(8,128)(2,1)S(1)}, u32[]{:S(2)}, u32[]{:S(2)}) %collective-permute-start.1) | collective-permute-done | bytes 262176 | tf_op jit(solution)/shard_map/ppermute | solution.py:26
  39.5 1.6 collective-permute-start.3
  41.2 22.6 %forward_chunk.2 = (bf16[512,7168]{1,0:T(8,128)(2,1)}, bf16[512,7168]{1,0:T(8,128)(2,1)}, bf16[3584,768]{1,0:T(8,128)(2,1)}, f32[512,256]{1,0:T(8,128)}) custom-call(s32[56,4]{1,0:T(8,128)} %copy.15.pattern_ref, s32[10]{0:T(128)} %stack.39.place_ref, bf16[512,2048]{1,0:T(8,128)(2,1)} %tokens_ref.1, bf16[512,1024]{1,0:T(8,128)(2,1)} %collective-permute-done.4.refs_1_, ...), custom_call_target="tpu_custom_call" | custom-call | flops 30000001024 | bytes 25165824 | tf_op jit(solution)/shard_map/forward_chunk/pallas_call | solution.py:112
  63.9 9.8 %spread.3 = bf16[512,2048]{1,0:T(8,128)(2,1)} custom-call(s32[56,4]{1,0:T(8,128)} %copy.15.pattern_ref, s32[10]{0:T(128)} %stack.39.place_ref, bf16[512,7168]{1,0:T(8,128)(2,1)} %get-tuple-element.65.grad_ref.refs_9_, bf16[7168,512]{1,0:T(8,128)(2,1)} %weight_ref.5), custom_call_target="tpu_custom_call" | custom-call | flops 30000001024 | bytes 25165824 | tf_op jit(solution)/shard_map/spread/pallas_call | solution.py:176
  73.7 4.6 %pair_sums.2 = (bf16[896,768]{1,0:T(8,128)(2,1)}, bf16[896,768]{1,0:T(8,128)(2,1)}) custom-call(s32[10]{0:T(128)} %stack.39.place_ref, bf16[3584,768]{1,0:T(8,128)(2,1)} %get-tuple-element.64.refs_0_.refs_1_, bf16[3584,768]{1,0:T(8,128)(2,1)} %get-tuple-element.64.refs_0_.refs_1_, bf16[3584,768]{1,0:T(8,128)(2,1)} %collective-permute-done.6.refs_2_.refs_3_, ...), custom_call_target="tpu_custom_call" | custom-call | tf_op jit(solution)/shard_map/pair_sums/pallas_call | solution.py:263
  78.3 3.6 %collective-permute-start.7 = (bf16[896,768]{1,0:T(8,128)(2,1)}, bf16[896,768]{1,0:T(8,128)(2,1)S(1)}, u32[]{:S(2)}, u32[]{:S(2)}) collective-permute-start(bf16[896,768]{1,0:T(8,128)(2,1)} %get-tuple-element.71), channel_id=1, source_target_pairs={{0,2},{1,3},{6,4},{7,5},{8,10},{9,11},{14,12},{15,13},{16,18},{17,... | collective-permute-start | bytes 4128776 | tf_op jit(solution)/shard_map/ppermute | solution.py:383
  81.9 3.6 %all-to-all-start = ((bf16[4,128,2048]{2,1,0:T(8,128)(2,1)}), bf16[4,128,2048]{2,1,0:T(8,128)(2,1)S(1)}, u32[]{:S(2)}, u32[]{:S(2)}) async-start(bf16[4,128,2048]{2,1,0:T(8,128)(2,1)} %bitcast.31), calls=%async_computation | async-start | bytes 4194304 | tf_op jit(solution)/shard_map/all_to_all | solution.py:359
  85.5 22.6 %forward_chunk.3 = (bf16[512,7168]{1,0:T(8,128)(2,1)}, bf16[512,7168]{1,0:T(8,128)(2,1)}, bf16[3584,768]{1,0:T(8,128)(2,1)}, f32[512,256]{1,0:T(8,128)}) custom-call(s32[56,4]{1,0:T(8,128)} %copy.15.pattern_ref, s32[10]{0:T(128)} %stack.39.place_ref, bf16[512,2048]{1,0:T(8,128)(2,1)} %tokens_ref.1, ...), custom_call_target="tpu_custom_call", output_to_operand_aliasing={{0}: (10, {}), {1}: (11, {})} | custom-call | flops 30000001024 | bytes 25165824 | tf_op jit(solution)/shard_map/forward_chunk/pallas_call | solution.py:112
  108.1 4.1 %collective-permute-done.7 = bf16[896,768]{1,0:T(8,128)(2,1)S(1)} collective-permute-done((bf16[896,768]{1,0:T(8,128)(2,1)}, bf16[896,768]{1,0:T(8,128)(2,1)S(1)}, u32[]{:S(2)}, u32[]{:S(2)}) %collective-permute-start.7) | collective-permute-done | bytes 1376288 | tf_op jit(solution)/shard_map/ppermute | solution.py:383
  112.2 5.5 %collective-permute-start.13 = (bf16[896,768]{1,0:T(8,128)(2,1)}, bf16[896,768]{1,0:T(8,128)(2,1)}, u32[]{:S(2)}, u32[]{:S(2)}) collective-permute-start(bf16[896,768]{1,0:T(8,128)(2,1)} %get-tuple-element.84), channel_id=1, source_target_pairs={{0,2},{1,3},{6,4},{7,5},{8,10},{9,11},{14,12},{15,13},{16,18},{17,... | collective-permute-start | bytes 4128776 | tf_op jit(solution)/shard_map/ppermute | solution.py:383
  119.0 1.6 collective-permute-start.10
  122.5 9.8 %spread.4 = bf16[512,2048]{1,0:T(8,128)(2,1)} custom-call(s32[56,4]{1,0:T(8,128)} %copy.15.pattern_ref, s32[10]{0:T(128)} %stack.39.place_ref, bf16[512,7168]{1,0:T(8,128)(2,1)} %get-tuple-element.77.grad_ref, bf16[7168,512]{1,0:T(8,128)(2,1)} %weight_ref.5), custom_call_target="tpu_custom_call" | custom-call | flops 30000001024 | bytes 25165824 | tf_op jit(solution)/shard_map/spread/pallas_call | solution.py:176
  132.4 2.8 %add_convert_fusion.2 = bf16[896,768]{1,0:T(8,128)(2,1)} fusion(bf16[896,768]{1,0:T(8,128)(2,1)S(1)} %copy-done.6, bf16[896,768]{1,0:T(8,128)(2,1)} %get-tuple-element.84), kind=kLoop, calls=%fused_computation.2 | loop fusion | flops 2752512 | bytes 4128768 | tf_op jit(solution)/shard_map/convert_element_type | solution.py:405
  135.2 1.7 collective-permute-start.14
  136.9 4.8 %pair_sums.3 = (bf16[896,768]{1,0:T(8,128)(2,1)}, f32[896,768]{1,0:T(8,128)}) custom-call(s32[10]{0:T(128)} %stack.39.place_ref, bf16[3584,768]{1,0:T(8,128)(2,1)} %get-tuple-element.74.refs_0_.refs_1_, bf16[3584,768]{1,0:T(8,128)(2,1)} %get-tuple-element.74.refs_0_.refs_1_, bf16[3584,768]{1,0:T(8,128)(2,1)} %collective-permute-done.8.refs_2_.refs_3_, ...), custom_call_target="tpu_custom_call" | custom-call | tf_op jit(solution)/shard_map/pair_sums/pallas_call | solution.py:263
  142.6 4.0 %right_sums.1 = (bf16[2,512,256]{2,1,0:T(8,128)(2,1)}, bf16[2,512,256]{2,1,0:T(8,128)(2,1)}) custom-call(s32[10]{0:T(128)} %stack.39.place_ref, bf16[512,2048]{1,0:T(8,128)(2,1)} %tokens_ref.1, bf16[512,256]{1,0:T(8,128)(2,1)} %add_convert_fusion.4.refs_0_.back_ref), custom_call_target="tpu_custom_call" | custom-call | tf_op jit(solution)/shard_map/right_sums/pallas_call | solution.py:235
  146.8 3.6 %all-to-all-start.2 = ((bf16[4,128,2048]{2,1,0:T(8,128)(2,1)}), bf16[4,128,2048]{2,1,0:T(8,128)(2,1)S(1)}, u32[]{:S(2)}, u32[]{:S(2)}) async-start(bf16[4,128,2048]{2,1,0:T(8,128)(2,1)} %bitcast.30), calls=%async_computation.2 | async-start | bytes 4194304 | tf_op jit(solution)/shard_map/all_to_all | solution.py:359
  150.4 16.4 %spread.5 = bf16[512,2048]{1,0:T(8,128)(2,1)} custom-call(s32[56,4]{1,0:T(8,128)} %copy.15.pattern_ref, s32[10]{0:T(128)} %stack.39.place_ref, bf16[512,7168]{1,0:T(8,128)(2,1)} %get-tuple-element.77.grad_ref, bf16[7168,512]{1,0:T(8,128)(2,1)} %weight_ref.5, bf16[512,256]{1,0:T(8,128)(2,1)} %add_convert_fusion.4.refs_0_.back_ref, bf16[2048,256]{1,0:T(8,128)(2,1)} %refs_1_.1, ...), custom_call_target="tpu_custom_call" | custom-call | flops 30000001024 | bytes 25165824 | tf_op jit(solution)/shard_map/spread/pallas_call | solution.py:176
  167.7 2.9 %collective-permute-start.15 = (bf16[512,256]{1,0:T(8,128)(2,1)}, bf16[512,256]{1,0:T(8,128)(2,1)}, u32[]{:S(2)}, u32[]{:S(2)}) collective-permute-start(bf16[512,256]{1,0:T(8,128)(2,1)} %fusion.1), channel_id=1, source_target_pairs={{0,4},{1,5},{2,6},{3,7},{4,0},{5,1},{6,2},{7,3},{8,12},{9,13},{10,... | collective-permute-start | bytes 786440 | tf_op jit(solution)/shard_map/ppermute | solution.py:26
  170.6 4.3 %all-to-all-done.2.refs_1_ = bf16[4,128,2048]{2,1,0:T(8,128)(2,1)S(1)} async-done(((bf16[4,128,2048]{2,1,0:T(8,128)(2,1)}), bf16[4,128,2048]{2,1,0:T(8,128)(2,1)S(1)}, u32[]{:S(2)}, u32[]{:S(2)}) %all-to-all-start.2) | async-done | bytes 2097184 | tf_op jit(solution)/shard_map/all_to_all | solution.py:359
  176.2 4.5 %all-to-all-start.1 = ((bf16[4,128,2048]{2,1,0:T(8,128)(2,1)}), bf16[4,128,2048]{2,1,0:T(8,128)(2,1)}, u32[]{:S(2)}, u32[]{:S(2)}) async-start(bf16[4,128,2048]{2,1,0:T(8,128)(2,1)} %bitcast.29), calls=%async_computation.1 | async-start | bytes 4194304 | tf_op jit(solution)/shard_map/all_to_all | solution.py:359
  180.7 4.4 %add_convert_fusion = (bf16[896,768]{1,0:T(8,128)(2,1)}, bf16[896,768]{1,0:T(8,128)(2,1)}) fusion(bf16[896,768]{1,0:T(8,128)(2,1)} %collective-permute-done.13, bf16[896,768]{1,0:T(8,128)(2,1)S(1)} %copy-done.7, bf16[896,768]{1,0:T(8,128)(2,1)} %collective-permute-done.14, bf16[896,768]{1,0:T(8,128)(2,1)} %get-tuple-element.91), kind=kLoop, calls=%fused_computation | loop fusion | flops 5505024 | bytes 8257536 | tf_op jit(solution)/shard_map/convert_element_type | solution.py:426
  185.8 4.5 %collective-permute-start.18 = (bf16[896,768]{1,0:T(8,128)(2,1)}, bf16[896,768]{1,0:T(8,128)(2,1)S(1)}, u32[]{:S(2)}, u32[]{:S(2)}) collective-permute-start(bf16[896,768]{1,0:T(8,128)(2,1)} %get-tuple-element.96), channel_id=1, source_target_pairs={{0,2},{1,3},{2,0},{3,1},{4,6},{5,7},{6,4},{7,5},{8,10},{9,11},{10,... | collective-permute-start | bytes 4128776 | tf_op jit(solution)/shard_map/ppermute | solution.py:26
  193.7 11.3 %all-to-all-done.1.own_ref = bf16[4,128,2048]{2,1,0:T(8,128)(2,1)} async-done(((bf16[4,128,2048]{2,1,0:T(8,128)(2,1)}), bf16[4,128,2048]{2,1,0:T(8,128)(2,1)}, u32[]{:S(2)}, u32[]{:S(2)}) %all-to-all-start.1) | async-done | bytes 2097184 | tf_op jit(solution)/shard_map/all_to_all | solution.py:359
  205.0 5.7 %merge_terms.1 = bf16[1,128,8192]{2,1,0:T(8,128)(2,1)} custom-call(s32[10]{0:T(128)} %stack.39.place_ref, bf16[4,128,2048]{2,1,0:T(8,128)(2,1)} %all-to-all-done.1.own_ref, bf16[4,128,2048]{2,1,0:T(8,128)(2,1)} %copy-done.1, bf16[4,128,2048]{2,1,0:T(8,128)(2,1)} %copy-done.2), custom_call_target="tpu_custom_call" | custom-call | tf_op jit(solution)/shard_map/merge_terms/pallas_call | solution.py:210
  210.7 9.0 %collective-permute-done.18.second_ref = bf16[896,768]{1,0:T(8,128)(2,1)S(1)} collective-permute-done((bf16[896,768]{1,0:T(8,128)(2,1)}, bf16[896,768]{1,0:T(8,128)(2,1)S(1)}, u32[]{:S(2)}, u32[]{:S(2)}) %collective-permute-start.18) | collective-permute-done | bytes 1376288 | tf_op jit(solution)/shard_map/ppermute | solution.py:26
  220.8 3.8 %final_sums.1 = (f32[896,512]{1,0:T(8,128)}, f32[896,256]{1,0:T(8,128)}) custom-call(f32[896,768]{1,0:T(8,128)} %get-tuple-element.82.refs_2_.kept_ref, bf16[896,768]{1,0:T(8,128)(2,1)} %copy-done.3, bf16[896,768]{1,0:T(8,128)(2,1)} %copy-done.4), custom_call_target="tpu_custom_call" | custom-call | tf_op jit(solution)/shard_map/final_sums/pallas_call | solution.py:291
  (64 shorter events, 17.3 us)
Async XLA Ops:
  3.4 9.3 %collective-permute-start = (bf16[512,256]{1,0:T(8,128)(2,1)S(1)}, bf16[512,256]{1,0:T(8,128)(2,1)S(1)}, u32[]{:S(2)}, u32[]{:S(2)}) collective-permute-start(bf16[512,256]{1,0:T(8,128)(2,1)S(1)} %get-tuple-element.107), channel_id=1, source_target_pairs={{0,16},{8,24},{16,0},{24,8},{1,17},{9,25},{17,1},{25,9},{2,18},{10... | collective-permute-start | bytes 786440 | tf_op jit(solution)/shard_map/ppermute | solution.py:26
  6.4 9.7 %copy-start.11 = (s32[56,4]{0,1:T(4,128)S(1)}, s32[56,4]{0,1:T(4,128)}, u32[]{:S(2)}) copy-start(s32[56,4]{0,1:T(4,128)} %param.10) | copy-start | bytes 2692
  7.9 31.2 %copy-start.8 = (bf16[512,1024]{1,0:T(8,128)(2,1)S(1)}, bf16[512,1024]{1,0:T(8,128)(2,1)}, u32[]{:S(2)}) copy-start(bf16[512,1024]{1,0:T(8,128)(2,1)} %get-tuple-element.55) | copy-start | bytes 3145732
  7.9 33.2 %collective-permute-start.5 = (bf16[512,1024]{1,0:T(8,128)(2,1)}, bf16[512,1024]{1,0:T(8,128)(2,1)}, u32[]{:S(2)}, u32[]{:S(2)}) collective-permute-start(bf16[512,1024]{1,0:T(8,128)(2,1)} %get-tuple-element.56), channel_id=1, source_target_pairs={{0,8},{8,0},{16,24},{24,16},{1,9},{9,1},{17,25},{25,17},{2,10},{10... | collective-permute-start | bytes 3145736 | tf_op jit(solution)/shard_map/ppermute | solution.py:26
  12.7 28.5 %collective-permute-start.4 = (bf16[512,1024]{1,0:T(8,128)(2,1)}, bf16[512,1024]{1,0:T(8,128)(2,1)}, u32[]{:S(2)}, u32[]{:S(2)}) collective-permute-start(bf16[512,1024]{1,0:T(8,128)(2,1)} %get-tuple-element.56), channel_id=1, source_target_pairs={{0,16},{8,24},{16,0},{24,8},{1,17},{9,25},{17,1},{25,9},{2,18},{10... | collective-permute-start | bytes 3145736 | tf_op jit(solution)/shard_map/ppermute | solution.py:26
  14.5 23.9 %collective-permute-start.1 = (bf16[512,256]{1,0:T(8,128)(2,1)S(1)}, bf16[512,256]{1,0:T(8,128)(2,1)S(1)}, u32[]{:S(2)}, u32[]{:S(2)}) collective-permute-start(bf16[512,256]{1,0:T(8,128)(2,1)S(1)} %fusion), channel_id=1, source_target_pairs={{0,8},{8,0},{16,24},{24,16},{1,9},{9,1},{17,25},{25,17},{2,10},{10... | collective-permute-start | bytes 786440 | tf_op jit(solution)/shard_map/ppermute | solution.py:26
  39.2 24.6 %collective-permute-start.2 = (bf16[512,1024]{1,0:T(8,128)(2,1)S(1)}, bf16[512,1024]{1,0:T(8,128)(2,1)S(1)}, u32[]{:S(2)}, u32[]{:S(2)}) collective-permute-start(bf16[512,1024]{1,0:T(8,128)(2,1)S(1)} %copy-done.8), channel_id=1, source_target_pairs={{0,16},{8,24},{16,0},{24,8},{1,17},{9,25},{17,1},{25,9},{2,18},{10... | collective-permute-start | bytes 3145736 | tf_op jit(solution)/shard_map/ppermute | solution.py:26
  39.5 24.3 %collective-permute-start.3 = (bf16[512,1024]{1,0:T(8,128)(2,1)S(1)}, bf16[512,1024]{1,0:T(8,128)(2,1)S(1)}, u32[]{:S(2)}, u32[]{:S(2)}) collective-permute-start(bf16[512,1024]{1,0:T(8,128)(2,1)S(1)} %copy-done.8), channel_id=1, source_target_pairs={{0,8},{8,0},{16,24},{24,16},{1,9},{9,1},{17,25},{25,17},{2,10},{10... | collective-permute-start | bytes 3145736 | tf_op jit(solution)/shard_map/ppermute | solution.py:26
  63.8 9.9 %copy-start.12 = (bf16[512,1024]{1,0:T(8,128)(2,1)}, bf16[512,1024]{1,0:T(8,128)(2,1)S(1)}, u32[]{:S(2)}) copy-start(bf16[512,1024]{1,0:T(8,128)(2,1)S(1)} %collective-permute-done.2.refs_1_) | copy-start | bytes 3145732
  63.8 9.9 %copy-start.13 = (bf16[512,1024]{1,0:T(8,128)(2,1)}, bf16[512,1024]{1,0:T(8,128)(2,1)S(1)}, u32[]{:S(2)}) copy-start(bf16[512,1024]{1,0:T(8,128)(2,1)S(1)} %collective-permute-done.3.refs_2_) | copy-start | bytes 3145732
  63.8 9.9 %collective-permute-start.6 = (bf16[3584,768]{1,0:T(8,128)(2,1)}, bf16[3584,768]{1,0:T(8,128)(2,1)}, u32[]{:S(2)}, u32[]{:S(2)}) collective-permute-start(bf16[3584,768]{1,0:T(8,128)(2,1)} %get-tuple-element.64.refs_0_.refs_1_), channel_id=1, source_target_pairs={{0,1},{1,0},{2,3},{3,2},{4,5},{5,4},{6,7},{7,6},{8,9},{9,8},{10,11... | collective-permute-start | bytes 16515080 | tf_op jit(solution)/shard_map/ppermute | solution.py:26
  78.3 33.9 %collective-permute-start.7 = (bf16[896,768]{1,0:T(8,128)(2,1)}, bf16[896,768]{1,0:T(8,128)(2,1)S(1)}, u32[]{:S(2)}, u32[]{:S(2)}) collective-permute-start(bf16[896,768]{1,0:T(8,128)(2,1)} %get-tuple-element.71), channel_id=1, source_target_pairs={{0,2},{1,3},{6,4},{7,5},{8,10},{9,11},{14,12},{15,13},{16,18},{17,... | collective-permute-start | bytes 4128776 | tf_op jit(solution)/shard_map/ppermute | solution.py:383
  81.9 30.3 %all-to-all-start = ((bf16[4,128,2048]{2,1,0:T(8,128)(2,1)}), bf16[4,128,2048]{2,1,0:T(8,128)(2,1)S(1)}, u32[]{:S(2)}, u32[]{:S(2)}) async-start(bf16[4,128,2048]{2,1,0:T(8,128)(2,1)} %bitcast.31), calls=%async_computation | async-start | bytes 4194304 | tf_op jit(solution)/shard_map/all_to_all | solution.py:359
  112.2 20.2 %copy-start.1 = (bf16[4,128,2048]{2,1,0:T(8,128)(2,1)}, bf16[4,128,2048]{2,1,0:T(8,128)(2,1)S(1)}, u32[]{:S(2)}) copy-start(bf16[4,128,2048]{2,1,0:T(8,128)(2,1)S(1)} %all-to-all-done.refs_0_) | copy-start | bytes 6291460
  112.2 24.7 %collective-permute-start.8 = (bf16[3584,768]{1,0:T(8,128)(2,1)}, bf16[3584,768]{1,0:T(8,128)(2,1)}, u32[]{:S(2)}, u32[]{:S(2)}) collective-permute-start(bf16[3584,768]{1,0:T(8,128)(2,1)} %get-tuple-element.74.refs_0_.refs_1_), channel_id=1, source_target_pairs={{0,1},{1,0},{2,3},{3,2},{4,5},{5,4},{6,7},{7,6},{8,9},{9,8},{10,11... | collective-permute-start | bytes 16515080 | tf_op jit(solution)/shard_map/ppermute | solution.py:26
  112.2 54.6 %collective-permute-start.13 = (bf16[896,768]{1,0:T(8,128)(2,1)}, bf16[896,768]{1,0:T(8,128)(2,1)}, u32[]{:S(2)}, u32[]{:S(2)}) collective-permute-start(bf16[896,768]{1,0:T(8,128)(2,1)} %get-tuple-element.84), channel_id=1, source_target_pairs={{0,2},{1,3},{6,4},{7,5},{8,10},{9,11},{14,12},{15,13},{16,18},{17,... | collective-permute-start | bytes 4128776 | tf_op jit(solution)/shard_map/ppermute | solution.py:383
  119.0 13.4 %copy-start.6 = (bf16[896,768]{1,0:T(8,128)(2,1)S(1)}, bf16[896,768]{1,0:T(8,128)(2,1)}, u32[]{:S(2)}) copy-start(bf16[896,768]{1,0:T(8,128)(2,1)} %copy-done.5) | copy-start | bytes 4128772
  119.0 16.2 %collective-permute-start.10 = (bf16[512,256]{1,0:T(8,128)(2,1)S(1)}, bf16[512,256]{1,0:T(8,128)(2,1)S(1)}, u32[]{:S(2)}, u32[]{:S(2)}) collective-permute-start(bf16[512,256]{1,0:T(8,128)(2,1)S(1)} %get-tuple-element.103), channel_id=1, source_target_pairs={{0,16},{8,24},{16,0},{24,8},{1,17},{9,25},{17,1},{25,9},{2,18},{10... | collective-permute-start | bytes 786440 | tf_op jit(solution)/shard_map/ppermute | solution.py:26
  120.6 16.4 %collective-permute-start.11 = (bf16[512,256]{1,0:T(8,128)(2,1)S(1)}, bf16[512,256]{1,0:T(8,128)(2,1)S(1)}, u32[]{:S(2)}, u32[]{:S(2)}) collective-permute-start(bf16[512,256]{1,0:T(8,128)(2,1)S(1)} %get-tuple-element.103), channel_id=1, source_target_pairs={{0,24},{8,16},{16,8},{24,0},{1,25},{9,17},{17,9},{25,1},{2,26},{10... | collective-permute-start | bytes 786440 | tf_op jit(solution)/shard_map/ppermute | solution.py:26
  121.3 15.6 %collective-permute-start.9 = (bf16[512,256]{1,0:T(8,128)(2,1)S(1)}, bf16[512,256]{1,0:T(8,128)(2,1)S(1)}, u32[]{:S(2)}, u32[]{:S(2)}) collective-permute-start(bf16[512,256]{1,0:T(8,128)(2,1)S(1)} %get-tuple-element.103), channel_id=1, source_target_pairs={{0,8},{8,0},{16,24},{24,16},{1,9},{9,1},{17,25},{25,17},{2,10},{10... | collective-permute-start | bytes 786440 | tf_op jit(solution)/shard_map/ppermute | solution.py:26
  135.2 31.7 %collective-permute-start.14 = (bf16[896,768]{1,0:T(8,128)(2,1)}, bf16[896,768]{1,0:T(8,128)(2,1)}, u32[]{:S(2)}, u32[]{:S(2)}) collective-permute-start(bf16[896,768]{1,0:T(8,128)(2,1)} %add_convert_fusion.2), channel_id=1, source_target_pairs={{2,4},{3,5},{4,2},{5,3},{10,12},{11,13},{12,10},{13,11},{18,20},{1... | collective-permute-start | bytes 4128776 | tf_op jit(solution)/shard_map/ppermute | solution.py:383
  146.6 20.3 %collective-permute-start.12 = (bf16[2,512,256]{2,1,0:T(8,128)(2,1)}, bf16[2,512,256]{2,1,0:T(8,128)(2,1)S(1)}, u32[]{:S(2)}, u32[]{:S(2)}) collective-permute-start(bf16[2,512,256]{2,1,0:T(8,128)(2,1)} %get-tuple-element.83), channel_id=1, source_target_pairs={{0,2},{1,3},{2,0},{3,1},{4,6},{5,7},{6,4},{7,5},{8,10},{9,11},{10,... | collective-permute-start | bytes 1572872 | tf_op jit(solution)/shard_map/ppermute | solution.py:26
  146.8 28.1 %all-to-all-start.2 = ((bf16[4,128,2048]{2,1,0:T(8,128)(2,1)}), bf16[4,128,2048]{2,1,0:T(8,128)(2,1)S(1)}, u32[]{:S(2)}, u32[]{:S(2)}) async-start(bf16[4,128,2048]{2,1,0:T(8,128)(2,1)} %bitcast.30), calls=%async_computation.2 | async-start | bytes 4194304 | tf_op jit(solution)/shard_map/all_to_all | solution.py:359
  150.4 16.5 %copy-start.9 = (bf16[2,512,256]{2,1,0:T(8,128)(2,1)S(1)}, bf16[2,512,256]{2,1,0:T(8,128)(2,1)}, u32[]{:S(2)}) copy-start(bf16[2,512,256]{2,1,0:T(8,128)(2,1)} %get-tuple-element.89) | copy-start | bytes 1572868
  166.8 8.0 %copy-start.10 = (bf16[2,512,256]{2,1,0:T(8,128)(2,1)}, bf16[2,512,256]{2,1,0:T(8,128)(2,1)S(1)}, u32[]{:S(2)}) copy-start(bf16[2,512,256]{2,1,0:T(8,128)(2,1)S(1)} %collective-permute-done.12) | copy-start | bytes 1572868
  167.7 17.3 %collective-permute-start.15 = (bf16[512,256]{1,0:T(8,128)(2,1)}, bf16[512,256]{1,0:T(8,128)(2,1)}, u32[]{:S(2)}, u32[]{:S(2)}) collective-permute-start(bf16[512,256]{1,0:T(8,128)(2,1)} %fusion.1), channel_id=1, source_target_pairs={{0,4},{1,5},{2,6},{3,7},{4,0},{5,1},{6,2},{7,3},{8,12},{9,13},{10,... | collective-permute-start | bytes 786440 | tf_op jit(solution)/shard_map/ppermute | solution.py:26
  174.9 5.8 %copy-start.7 = (bf16[896,768]{1,0:T(8,128)(2,1)S(1)}, bf16[896,768]{1,0:T(8,128)(2,1)}, u32[]{:S(2)}) copy-start(bf16[896,768]{1,0:T(8,128)(2,1)} %get-tuple-element.71) | copy-start | bytes 4128772
  176.2 28.8 %all-to-all-start.1 = ((bf16[4,128,2048]{2,1,0:T(8,128)(2,1)}), bf16[4,128,2048]{2,1,0:T(8,128)(2,1)}, u32[]{:S(2)}, u32[]{:S(2)}) async-start(bf16[4,128,2048]{2,1,0:T(8,128)(2,1)} %bitcast.29), calls=%async_computation.1 | async-start | bytes 4194304 | tf_op jit(solution)/shard_map/all_to_all | solution.py:359
  185.1 25.7 %collective-permute-start.17 = (bf16[896,768]{1,0:T(8,128)(2,1)}, bf16[896,768]{1,0:T(8,128)(2,1)S(1)}, u32[]{:S(2)}, u32[]{:S(2)}) collective-permute-start(bf16[896,768]{1,0:T(8,128)(2,1)} %get-tuple-element.95), channel_id=1, source_target_pairs={{2,4},{3,5},{4,2},{5,3},{10,12},{11,13},{12,10},{13,11},{18,20},{1... | collective-permute-start | bytes 4128776 | tf_op jit(solution)/shard_map/ppermute | solution.py:383
  185.8 33.9 %collective-permute-start.18 = (bf16[896,768]{1,0:T(8,128)(2,1)}, bf16[896,768]{1,0:T(8,128)(2,1)S(1)}, u32[]{:S(2)}, u32[]{:S(2)}) collective-permute-start(bf16[896,768]{1,0:T(8,128)(2,1)} %get-tuple-element.96), channel_id=1, source_target_pairs={{0,2},{1,3},{2,0},{3,1},{4,6},{5,7},{6,4},{7,5},{8,10},{9,11},{10,... | collective-permute-start | bytes 4128776 | tf_op jit(solution)/shard_map/ppermute | solution.py:26
  191.6 1.4 collective-permute-start.16
  210.7 9.0 %copy-start.3 = (bf16[896,768]{1,0:T(8,128)(2,1)}, bf16[896,768]{1,0:T(8,128)(2,1)S(1)}, u32[]{:S(2)}) copy-start(bf16[896,768]{1,0:T(8,128)(2,1)S(1)} %collective-permute-done.17.first_ref) | copy-start | bytes 4128772
  (4 other events, 13.7 us)

commit v3 on v2

--- a/solution.py
+++ b/solution.py
@@ -421,9 +421,10 @@
     own, close, got1, got2 = hold((own, close, got1, got2))
 
     last_part = far_hop((wide(right_keep[0]) + wide(close[0])).astype(BF16))
-    own = to_owner(own)
     send4 = (wide(sum2) + wide(got2)).astype(BF16)
     send3 = (wide(sum0) + wide(got1)).astype(BF16)
+    own, send4, send3 = hold((own, send4, send3))
+    own = to_owner(own)
     send4, send3, last_part = hold((send4, send3, last_part))
     got4 = near_hop(send4)
     got3 = across(send3)

time: 226 us -> 222 us (0.982)
  waiting for transfers between devices: 54.3 us -> 51.4 us
    ppermute x15, waiting for transfers between devices: 34.6 us -> 30.6 us  [from_partner(): return lax.ppermute(value, axis, pairs)]
  transfers between devices with their start and end apart: 22 -> 22, of which waited for: 7 -> 8; matrix products, arithmetic and copies ran while one was open for 7% -> 7% of each run, Pallas kernels for 43% -> 44%
where the time goes in v3:
time: 222 us; the launch traced here: 220 us
  Pallas kernels  104 us (47%)
  waiting for transfers between devices  51.4 us (23%)
  starting transfers between devices  44 us (20%)
  other arithmetic  11.6 us (5%)
  local copies, waits for them, and re-layouts  5.35 us (2%)
  matrix products  2.71 us (1%)
    pallas_call x2, Pallas kernels, forward_chunk(): pl.pallas_call(functools.partial(forward_kernel, turn, width), grid_spec=...  45.3 us
    pallas_call x3, Pallas kernels, spread(): pl.pallas_call(functools.partial(spread_kernel, turn, steps, width, tuple...  36.1 us
    ppermute x15, waiting for transfers between devices, from_partner(): return lax.ppermute(value, axis, pairs)  30.6 us
    ppermute x15, starting transfers between devices, from_partner(): return lax.ppermute(value, axis, pairs)  20.8 us
    all_to_all x3, waiting for transfers between devices, to_owner(): lax.all_to_all(value, 'feat', split_axis=0, concat_axis=0, tiled=True)  16.8 us
    all_to_all x3, starting transfers between devices, to_owner(): lax.all_to_all(value, 'feat', split_axis=0, concat_axis=0, tiled=True)  11.7 us
    ppermute x4, starting transfers between devices, line_hop(): return lax.ppermute(value, 'seq', pairs)  11.6 us
    pallas_call x2, Pallas kernels, pair_sums(): pl.pallas_call(pair_kernel, grid_spec=pltpu.PrefetchScalarGridSpec(num_sc...  9.38 us
  transfers between devices with their start and end apart: 22, of which 8 were waited for; matrix products, arithmetic and copies ran while one was open for 7% of the time, Pallas kernels for 44%

profile of v3, /device:TPU:0, one launch (start us, length us, event | category | flops | bytes accessed | tf_op | source)
XLA Modules:
  0.0 220.2 jit_solution(5930321244331248183)
XLA Ops:
  0.6 2.7 %fusion.6 = (bf16[512,256]{1,0:T(8,128)(2,1)S(1)}, f32[512,256]{1,0:T(8,128)S(1)}) fusion(bf16[512,2048]{1,0:T(8,128)(2,1)} %tokens_ref.1, bf16[2048,256]{1,0:T(8,128)(2,1)} %refs_1_.1), kind=kOutput, calls=%fused_computation.18 | convolution fusion | flops 537001984 | bytes 3932160 | tf_op jit(solution)/shard_map/dot_general | solution.py:330
  3.4 3.0 %collective-permute-start = (bf16[512,256]{1,0:T(8,128)(2,1)S(1)}, bf16[512,256]{1,0:T(8,128)(2,1)S(1)}, u32[]{:S(2)}, u32[]{:S(2)}) collective-permute-start(bf16[512,256]{1,0:T(8,128)(2,1)S(1)} %get-tuple-element.113), channel_id=1, source_target_pairs={{0,16},{8,24},{16,0},{24,8},{1,17},{9,25},{17,1},{25,9},{2,18},{10... | collective-permute-start | bytes 786440 | tf_op jit(solution)/shard_map/ppermute | solution.py:26
  6.4 1.5 constant_dynamic-slice_fusion
  9.4 3.3 %collective-permute-done = bf16[512,256]{1,0:T(8,128)(2,1)S(1)} collective-permute-done((bf16[512,256]{1,0:T(8,128)(2,1)S(1)}, bf16[512,256]{1,0:T(8,128)(2,1)S(1)}, u32[]{:S(2)}, u32[]{:S(2)}) %collective-permute-start) | collective-permute-done | bytes 262176 | tf_op jit(solution)/shard_map/ppermute | solution.py:26
  12.7 1.7 collective-permute-start.4
  14.5 1.6 collective-permute-start.1
  17.4 21.0 %collective-permute-done.1 = bf16[512,256]{1,0:T(8,128)(2,1)S(1)} collective-permute-done((bf16[512,256]{1,0:T(8,128)(2,1)S(1)}, bf16[512,256]{1,0:T(8,128)(2,1)S(1)}, u32[]{:S(2)}, u32[]{:S(2)}) %collective-permute-start.1) | collective-permute-done | bytes 262176 | tf_op jit(solution)/shard_map/ppermute | solution.py:26
  39.5 1.6 collective-permute-start.3
  41.2 22.6 %forward_chunk.2 = (bf16[512,7168]{1,0:T(8,128)(2,1)}, bf16[512,7168]{1,0:T(8,128)(2,1)}, bf16[3584,768]{1,0:T(8,128)(2,1)}, f32[512,256]{1,0:T(8,128)}) custom-call(s32[56,4]{1,0:T(8,128)} %copy.15.pattern_ref, s32[10]{0:T(128)} %stack.39.place_ref, bf16[512,2048]{1,0:T(8,128)(2,1)} %tokens_ref.1, bf16[512,1024]{1,0:T(8,128)(2,1)} %collective-permute-done.4.refs_1_, ...), custom_call_target="tpu_custom_call" | custom-call | flops 30000001024 | bytes 25165824 | tf_op jit(solution)/shard_map/forward_chunk/pallas_call | solution.py:112
  63.9 9.8 %spread.3 = bf16[512,2048]{1,0:T(8,128)(2,1)} custom-call(s32[56,4]{1,0:T(8,128)} %copy.15.pattern_ref, s32[10]{0:T(128)} %stack.39.place_ref, bf16[512,7168]{1,0:T(8,128)(2,1)} %get-tuple-element.68.grad_ref.refs_9_, bf16[7168,512]{1,0:T(8,128)(2,1)} %weight_ref.5), custom_call_target="tpu_custom_call" | custom-call | flops 30000001024 | bytes 25165824 | tf_op jit(solution)/shard_map/spread/pallas_call | solution.py:176
  73.7 4.6 %pair_sums.2 = (bf16[896,768]{1,0:T(8,128)(2,1)}, bf16[896,768]{1,0:T(8,128)(2,1)}) custom-call(s32[10]{0:T(128)} %stack.39.place_ref, bf16[3584,768]{1,0:T(8,128)(2,1)} %get-tuple-element.67.refs_0_.refs_1_, bf16[3584,768]{1,0:T(8,128)(2,1)} %get-tuple-element.67.refs_0_.refs_1_, bf16[3584,768]{1,0:T(8,128)(2,1)} %collective-permute-done.6.refs_2_.refs_3_, ...), custom_call_target="tpu_custom_call" | custom-call | tf_op jit(solution)/shard_map/pair_sums/pallas_call | solution.py:263
  78.3 3.6 %collective-permute-start.7 = (bf16[896,768]{1,0:T(8,128)(2,1)}, bf16[896,768]{1,0:T(8,128)(2,1)S(1)}, u32[]{:S(2)}, u32[]{:S(2)}) collective-permute-start(bf16[896,768]{1,0:T(8,128)(2,1)} %get-tuple-element.74), channel_id=1, source_target_pairs={{0,2},{1,3},{6,4},{7,5},{8,10},{9,11},{14,12},{15,13},{16,18},{17,... | collective-permute-start | bytes 4128776 | tf_op jit(solution)/shard_map/ppermute | solution.py:383
  81.9 3.6 %all-to-all-start = ((bf16[4,128,2048]{2,1,0:T(8,128)(2,1)}), bf16[4,128,2048]{2,1,0:T(8,128)(2,1)S(1)}, u32[]{:S(2)}, u32[]{:S(2)}) async-start(bf16[4,128,2048]{2,1,0:T(8,128)(2,1)} %bitcast.31), calls=%async_computation | async-start | bytes 4194304 | tf_op jit(solution)/shard_map/all_to_all | solution.py:359
  85.5 22.7 %forward_chunk.3 = (bf16[512,7168]{1,0:T(8,128)(2,1)}, bf16[512,7168]{1,0:T(8,128)(2,1)}, bf16[3584,768]{1,0:T(8,128)(2,1)}, f32[512,256]{1,0:T(8,128)}) custom-call(s32[56,4]{1,0:T(8,128)} %copy.15.pattern_ref, s32[10]{0:T(128)} %stack.39.place_ref, bf16[512,2048]{1,0:T(8,128)(2,1)} %tokens_ref.1, ...), custom_call_target="tpu_custom_call", output_to_operand_aliasing={{0}: (10, {}), {1}: (11, {})} | custom-call | flops 30000001024 | bytes 25165824 | tf_op jit(solution)/shard_map/forward_chunk/pallas_call | solution.py:112
  108.2 4.0 %collective-permute-done.7 = bf16[896,768]{1,0:T(8,128)(2,1)S(1)} collective-permute-done((bf16[896,768]{1,0:T(8,128)(2,1)}, bf16[896,768]{1,0:T(8,128)(2,1)S(1)}, u32[]{:S(2)}, u32[]{:S(2)}) %collective-permute-start.7) | collective-permute-done | bytes 1376288 | tf_op jit(solution)/shard_map/ppermute | solution.py:383
  112.2 5.5 %collective-permute-start.13 = (bf16[896,768]{1,0:T(8,128)(2,1)}, bf16[896,768]{1,0:T(8,128)(2,1)}, u32[]{:S(2)}, u32[]{:S(2)}) collective-permute-start(bf16[896,768]{1,0:T(8,128)(2,1)} %get-tuple-element.87), channel_id=1, source_target_pairs={{0,2},{1,3},{6,4},{7,5},{8,10},{9,11},{14,12},{15,13},{16,18},{17,... | collective-permute-start | bytes 4128776 | tf_op jit(solution)/shard_map/ppermute | solution.py:383
  119.0 1.6 collective-permute-start.10
  122.6 9.9 %spread.4 = bf16[512,2048]{1,0:T(8,128)(2,1)} custom-call(s32[56,4]{1,0:T(8,128)} %copy.15.pattern_ref, s32[10]{0:T(128)} %stack.39.place_ref, bf16[512,7168]{1,0:T(8,128)(2,1)} %get-tuple-element.80.grad_ref, bf16[7168,512]{1,0:T(8,128)(2,1)} %weight_ref.5), custom_call_target="tpu_custom_call" | custom-call | flops 30000001024 | bytes 25165824 | tf_op jit(solution)/shard_map/spread/pallas_call | solution.py:176
  132.5 2.8 %add_convert_fusion.2 = bf16[896,768]{1,0:T(8,128)(2,1)} fusion(bf16[896,768]{1,0:T(8,128)(2,1)S(1)} %copy-done.6, bf16[896,768]{1,0:T(8,128)(2,1)} %get-tuple-element.87), kind=kLoop, calls=%fused_computation.2 | loop fusion | flops 2752512 | bytes 4128768 | tf_op jit(solution)/shard_map/convert_element_type | solution.py:405
  135.2 1.7 collective-permute-start.14
  137.0 4.8 %pair_sums.3 = (bf16[896,768]{1,0:T(8,128)(2,1)}, f32[896,768]{1,0:T(8,128)}) custom-call(s32[10]{0:T(128)} %stack.39.place_ref, bf16[3584,768]{1,0:T(8,128)(2,1)} %get-tuple-element.77.refs_0_.refs_1_, bf16[3584,768]{1,0:T(8,128)(2,1)} %get-tuple-element.77.refs_0_.refs_1_, bf16[3584,768]{1,0:T(8,128)(2,1)} %collective-permute-done.8.refs_2_.refs_3_, ...), custom_call_target="tpu_custom_call" | custom-call | tf_op jit(solution)/shard_map/pair_sums/pallas_call | solution.py:263
  142.6 4.0 %right_sums.1 = (bf16[2,512,256]{2,1,0:T(8,128)(2,1)}, bf16[2,512,256]{2,1,0:T(8,128)(2,1)}) custom-call(s32[10]{0:T(128)} %stack.39.place_ref, bf16[512,2048]{1,0:T(8,128)(2,1)} %tokens_ref.1, bf16[512,256]{1,0:T(8,128)(2,1)} %add_convert_fusion.4.refs_0_.back_ref), custom_call_target="tpu_custom_call" | custom-call | tf_op jit(solution)/shard_map/right_sums/pallas_call | solution.py:235
  146.8 3.6 %all-to-all-start.2 = ((bf16[4,128,2048]{2,1,0:T(8,128)(2,1)}), bf16[4,128,2048]{2,1,0:T(8,128)(2,1)S(1)}, u32[]{:S(2)}, u32[]{:S(2)}) async-start(bf16[4,128,2048]{2,1,0:T(8,128)(2,1)} %bitcast.30), calls=%async_computation.2 | async-start | bytes 4194304 | tf_op jit(solution)/shard_map/all_to_all | solution.py:359
  150.5 16.5 %spread.5 = bf16[512,2048]{1,0:T(8,128)(2,1)} custom-call(s32[56,4]{1,0:T(8,128)} %copy.15.pattern_ref, s32[10]{0:T(128)} %stack.39.place_ref, bf16[512,7168]{1,0:T(8,128)(2,1)} %get-tuple-element.80.grad_ref, bf16[7168,512]{1,0:T(8,128)(2,1)} %weight_ref.5, bf16[512,256]{1,0:T(8,128)(2,1)} %add_convert_fusion.4.refs_0_.back_ref, bf16[2048,256]{1,0:T(8,128)(2,1)} %refs_1_.1, ...), custom_call_target="tpu_custom_call" | custom-call | flops 30000001024 | bytes 25165824 | tf_op jit(solution)/shard_map/spread/pallas_call | solution.py:176
  167.0 2.9 %collective-permute-start.15 = (bf16[512,256]{1,0:T(8,128)(2,1)S(1)}, bf16[512,256]{1,0:T(8,128)(2,1)S(1)}, u32[]{:S(2)}, u32[]{:S(2)}) collective-permute-start(bf16[512,256]{1,0:T(8,128)(2,1)S(1)} %fusion.1), channel_id=1, source_target_pairs={{0,4},{1,5},{2,6},{3,7},{4,0},{5,1},{6,2},{7,3},{8,12},{9,13},{10,... | collective-permute-start | bytes 786440 | tf_op jit(solution)/shard_map/ppermute | solution.py:26
  170.0 3.9 %add_convert_fusion = (bf16[896,768]{1,0:T(8,128)(2,1)}, bf16[896,768]{1,0:T(8,128)(2,1)}) fusion(bf16[896,768]{1,0:T(8,128)(2,1)} %collective-permute-done.13, bf16[896,768]{1,0:T(8,128)(2,1)S(1)} %copy-done.7, bf16[896,768]{1,0:T(8,128)(2,1)} %collective-permute-done.14, bf16[896,768]{1,0:T(8,128)(2,1)S(1)} %copy-done.8), kind=kLoop, calls=%fused_computation | loop fusion | flops 5505024 | bytes 8257536 | tf_op jit(solution)/shard_map/convert_element_type | solution.py:425
  176.2 4.5 %all-to-all-start.1 = ((bf16[4,128,2048]{2,1,0:T(8,128)(2,1)}), bf16[4,128,2048]{2,1,0:T(8,128)(2,1)}, u32[]{:S(2)}, u32[]{:S(2)}) async-start(bf16[4,128,2048]{2,1,0:T(8,128)(2,1)} %bitcast.29), calls=%async_computation.1 | async-start | bytes 4194304 | tf_op jit(solution)/shard_map/all_to_all | solution.py:359
  181.9 4.1 %collective-permute-start.18 = (bf16[896,768]{1,0:T(8,128)(2,1)}, bf16[896,768]{1,0:T(8,128)(2,1)S(1)}, u32[]{:S(2)}, u32[]{:S(2)}) collective-permute-start(bf16[896,768]{1,0:T(8,128)(2,1)} %get-tuple-element.102), channel_id=1, source_target_pairs={{0,2},{1,3},{2,0},{3,1},{4,6},{5,7},{6,4},{7,5},{8,10},{9,11},{10,... | collective-permute-start | bytes 4128776 | tf_op jit(solution)/shard_map/ppermute | solution.py:26
  189.3 15.8 %all-to-all-done.1.own_ref = bf16[4,128,2048]{2,1,0:T(8,128)(2,1)} async-done(((bf16[4,128,2048]{2,1,0:T(8,128)(2,1)}), bf16[4,128,2048]{2,1,0:T(8,128)(2,1)}, u32[]{:S(2)}, u32[]{:S(2)}) %all-to-all-start.1) | async-done | bytes 2097184 | tf_op jit(solution)/shard_map/all_to_all | solution.py:359
  205.1 5.7 %merge_terms.1 = bf16[1,128,8192]{2,1,0:T(8,128)(2,1)} custom-call(s32[10]{0:T(128)} %stack.39.place_ref, bf16[4,128,2048]{2,1,0:T(8,128)(2,1)} %all-to-all-done.1.own_ref, bf16[4,128,2048]{2,1,0:T(8,128)(2,1)} %copy-done.1, bf16[4,128,2048]{2,1,0:T(8,128)(2,1)} %copy-done.2), custom_call_target="tpu_custom_call" | custom-call | tf_op jit(solution)/shard_map/merge_terms/pallas_call | solution.py:210
  210.8 4.5 %collective-permute-done.18.second_ref = bf16[896,768]{1,0:T(8,128)(2,1)S(1)} collective-permute-done((bf16[896,768]{1,0:T(8,128)(2,1)}, bf16[896,768]{1,0:T(8,128)(2,1)S(1)}, u32[]{:S(2)}, u32[]{:S(2)}) %collective-permute-start.18) | collective-permute-done | bytes 1376288 | tf_op jit(solution)/shard_map/ppermute | solution.py:26
  216.4 3.8 %final_sums.1 = (f32[896,512]{1,0:T(8,128)}, f32[896,256]{1,0:T(8,128)}) custom-call(f32[896,768]{1,0:T(8,128)} %get-tuple-element.85.refs_2_.kept_ref, bf16[896,768]{1,0:T(8,128)(2,1)} %copy-done.3, bf16[896,768]{1,0:T(8,128)(2,1)} %copy-done.4), custom_call_target="tpu_custom_call" | custom-call | tf_op jit(solution)/shard_map/final_sums/pallas_call | solution.py:291
  (66 shorter events, 16.3 us)
Async XLA Ops:
  3.4 9.3 %collective-permute-start = (bf16[512,256]{1,0:T(8,128)(2,1)S(1)}, bf16[512,256]{1,0:T(8,128)(2,1)S(1)}, u32[]{:S(2)}, u32[]{:S(2)}) collective-permute-start(bf16[512,256]{1,0:T(8,128)(2,1)S(1)} %get-tuple-element.113), channel_id=1, source_target_pairs={{0,16},{8,24},{16,0},{24,8},{1,17},{9,25},{17,1},{25,9},{2,18},{10... | collective-permute-start | bytes 786440 | tf_op jit(solution)/shard_map/ppermute | solution.py:26
  6.4 9.7 %copy-start.12 = (s32[56,4]{0,1:T(4,128)S(1)}, s32[56,4]{0,1:T(4,128)}, u32[]{:S(2)}) copy-start(s32[56,4]{0,1:T(4,128)} %param.10) | copy-start | bytes 2692
  7.9 31.2 %copy-start.9 = (bf16[512,1024]{1,0:T(8,128)(2,1)S(1)}, bf16[512,1024]{1,0:T(8,128)(2,1)}, u32[]{:S(2)}) copy-start(bf16[512,1024]{1,0:T(8,128)(2,1)} %get-tuple-element.58) | copy-start | bytes 3145732
  7.9 33.2 %collective-permute-start.5 = (bf16[512,1024]{1,0:T(8,128)(2,1)}, bf16[512,1024]{1,0:T(8,128)(2,1)}, u32[]{:S(2)}, u32[]{:S(2)}) collective-permute-start(bf16[512,1024]{1,0:T(8,128)(2,1)} %get-tuple-element.59), channel_id=1, source_target_pairs={{0,8},{8,0},{16,24},{24,16},{1,9},{9,1},{17,25},{25,17},{2,10},{10... | collective-permute-start | bytes 3145736 | tf_op jit(solution)/shard_map/ppermute | solution.py:26
  12.7 28.5 %collective-permute-start.4 = (bf16[512,1024]{1,0:T(8,128)(2,1)}, bf16[512,1024]{1,0:T(8,128)(2,1)}, u32[]{:S(2)}, u32[]{:S(2)}) collective-permute-start(bf16[512,1024]{1,0:T(8,128)(2,1)} %get-tuple-element.59), channel_id=1, source_target_pairs={{0,16},{8,24},{16,0},{24,8},{1,17},{9,25},{17,1},{25,9},{2,18},{10... | collective-permute-start | bytes 3145736 | tf_op jit(solution)/shard_map/ppermute | solution.py:26
  14.5 23.9 %collective-permute-start.1 = (bf16[512,256]{1,0:T(8,128)(2,1)S(1)}, bf16[512,256]{1,0:T(8,128)(2,1)S(1)}, u32[]{:S(2)}, u32[]{:S(2)}) collective-permute-start(bf16[512,256]{1,0:T(8,128)(2,1)S(1)} %fusion), channel_id=1, source_target_pairs={{0,8},{8,0},{16,24},{24,16},{1,9},{9,1},{17,25},{25,17},{2,10},{10... | collective-permute-start | bytes 786440 | tf_op jit(solution)/shard_map/ppermute | solution.py:26
  39.2 24.6 %collective-permute-start.2 = (bf16[512,1024]{1,0:T(8,128)(2,1)S(1)}, bf16[512,1024]{1,0:T(8,128)(2,1)S(1)}, u32[]{:S(2)}, u32[]{:S(2)}) collective-permute-start(bf16[512,1024]{1,0:T(8,128)(2,1)S(1)} %copy-done.9), channel_id=1, source_target_pairs={{0,16},{8,24},{16,0},{24,8},{1,17},{9,25},{17,1},{25,9},{2,18},{10... | collective-permute-start | bytes 3145736 | tf_op jit(solution)/shard_map/ppermute | solution.py:26
  39.5 24.3 %collective-permute-start.3 = (bf16[512,1024]{1,0:T(8,128)(2,1)S(1)}, bf16[512,1024]{1,0:T(8,128)(2,1)S(1)}, u32[]{:S(2)}, u32[]{:S(2)}) collective-permute-start(bf16[512,1024]{1,0:T(8,128)(2,1)S(1)} %copy-done.9), channel_id=1, source_target_pairs={{0,8},{8,0},{16,24},{24,16},{1,9},{9,1},{17,25},{25,17},{2,10},{10... | collective-permute-start | bytes 3145736 | tf_op jit(solution)/shard_map/ppermute | solution.py:26
  63.8 9.9 %copy-start.13 = (bf16[512,1024]{1,0:T(8,128)(2,1)}, bf16[512,1024]{1,0:T(8,128)(2,1)S(1)}, u32[]{:S(2)}) copy-start(bf16[512,1024]{1,0:T(8,128)(2,1)S(1)} %collective-permute-done.2.refs_1_) | copy-start | bytes 3145732
  63.8 9.9 %copy-start.14 = (bf16[512,1024]{1,0:T(8,128)(2,1)}, bf16[512,1024]{1,0:T(8,128)(2,1)S(1)}, u32[]{:S(2)}) copy-start(bf16[512,1024]{1,0:T(8,128)(2,1)S(1)} %collective-permute-done.3.refs_2_) | copy-start | bytes 3145732
  63.8 9.9 %collective-permute-start.6 = (bf16[3584,768]{1,0:T(8,128)(2,1)}, bf16[3584,768]{1,0:T(8,128)(2,1)}, u32[]{:S(2)}, u32[]{:S(2)}) collective-permute-start(bf16[3584,768]{1,0:T(8,128)(2,1)} %get-tuple-element.67.refs_0_.refs_1_), channel_id=1, source_target_pairs={{0,1},{1,0},{2,3},{3,2},{4,5},{5,4},{6,7},{7,6},{8,9},{9,8},{10,11... | collective-permute-start | bytes 16515080 | tf_op jit(solution)/shard_map/ppermute | solution.py:26
  78.3 33.9 %collective-permute-start.7 = (bf16[896,768]{1,0:T(8,128)(2,1)}, bf16[896,768]{1,0:T(8,128)(2,1)S(1)}, u32[]{:S(2)}, u32[]{:S(2)}) collective-permute-start(bf16[896,768]{1,0:T(8,128)(2,1)} %get-tuple-element.74), channel_id=1, source_target_pairs={{0,2},{1,3},{6,4},{7,5},{8,10},{9,11},{14,12},{15,13},{16,18},{17,... | collective-permute-start | bytes 4128776 | tf_op jit(solution)/shard_map/ppermute | solution.py:383
  81.9 30.3 %all-to-all-start = ((bf16[4,128,2048]{2,1,0:T(8,128)(2,1)}), bf16[4,128,2048]{2,1,0:T(8,128)(2,1)S(1)}, u32[]{:S(2)}, u32[]{:S(2)}) async-start(bf16[4,128,2048]{2,1,0:T(8,128)(2,1)} %bitcast.31), calls=%async_computation | async-start | bytes 4194304 | tf_op jit(solution)/shard_map/all_to_all | solution.py:359
  112.2 20.2 %copy-start.1 = (bf16[4,128,2048]{2,1,0:T(8,128)(2,1)}, bf16[4,128,2048]{2,1,0:T(8,128)(2,1)S(1)}, u32[]{:S(2)}) copy-start(bf16[4,128,2048]{2,1,0:T(8,128)(2,1)S(1)} %all-to-all-done.refs_0_) | copy-start | bytes 6291460
  112.2 24.8 %collective-permute-start.8 = (bf16[3584,768]{1,0:T(8,128)(2,1)}, bf16[3584,768]{1,0:T(8,128)(2,1)}, u32[]{:S(2)}, u32[]{:S(2)}) collective-permute-start(bf16[3584,768]{1,0:T(8,128)(2,1)} %get-tuple-element.77.refs_0_.refs_1_), channel_id=1, source_target_pairs={{0,1},{1,0},{2,3},{3,2},{4,5},{5,4},{6,7},{7,6},{8,9},{9,8},{10,11... | collective-permute-start | bytes 16515080 | tf_op jit(solution)/shard_map/ppermute | solution.py:26
  112.2 54.7 %collective-permute-start.13 = (bf16[896,768]{1,0:T(8,128)(2,1)}, bf16[896,768]{1,0:T(8,128)(2,1)}, u32[]{:S(2)}, u32[]{:S(2)}) collective-permute-start(bf16[896,768]{1,0:T(8,128)(2,1)} %get-tuple-element.87), channel_id=1, source_target_pairs={{0,2},{1,3},{6,4},{7,5},{8,10},{9,11},{14,12},{15,13},{16,18},{17,... | collective-permute-start | bytes 4128776 | tf_op jit(solution)/shard_map/ppermute | solution.py:383
  119.0 13.4 %copy-start.6 = (bf16[896,768]{1,0:T(8,128)(2,1)S(1)}, bf16[896,768]{1,0:T(8,128)(2,1)}, u32[]{:S(2)}) copy-start(bf16[896,768]{1,0:T(8,128)(2,1)} %copy-done.5) | copy-start | bytes 4128772
  119.0 16.2 %collective-permute-start.10 = (bf16[512,256]{1,0:T(8,128)(2,1)S(1)}, bf16[512,256]{1,0:T(8,128)(2,1)S(1)}, u32[]{:S(2)}, u32[]{:S(2)}) collective-permute-start(bf16[512,256]{1,0:T(8,128)(2,1)S(1)} %get-tuple-element.109), channel_id=1, source_target_pairs={{0,16},{8,24},{16,0},{24,8},{1,17},{9,25},{17,1},{25,9},{2,18},{10... | collective-permute-start | bytes 786440 | tf_op jit(solution)/shard_map/ppermute | solution.py:26
  120.6 16.3 %collective-permute-start.11 = (bf16[512,256]{1,0:T(8,128)(2,1)S(1)}, bf16[512,256]{1,0:T(8,128)(2,1)S(1)}, u32[]{:S(2)}, u32[]{:S(2)}) collective-permute-start(bf16[512,256]{1,0:T(8,128)(2,1)S(1)} %get-tuple-element.109), channel_id=1, source_target_pairs={{0,24},{8,16},{16,8},{24,0},{1,25},{9,17},{17,9},{25,1},{2,26},{10... | collective-permute-start | bytes 786440 | tf_op jit(solution)/shard_map/ppermute | solution.py:26
  121.3 15.6 %collective-permute-start.9 = (bf16[512,256]{1,0:T(8,128)(2,1)S(1)}, bf16[512,256]{1,0:T(8,128)(2,1)S(1)}, u32[]{:S(2)}, u32[]{:S(2)}) collective-permute-start(bf16[512,256]{1,0:T(8,128)(2,1)S(1)} %get-tuple-element.109), channel_id=1, source_target_pairs={{0,8},{8,0},{16,24},{24,16},{1,9},{9,1},{17,25},{25,17},{2,10},{10... | collective-permute-start | bytes 786440 | tf_op jit(solution)/shard_map/ppermute | solution.py:26
  135.2 31.7 %collective-permute-start.14 = (bf16[896,768]{1,0:T(8,128)(2,1)}, bf16[896,768]{1,0:T(8,128)(2,1)}, u32[]{:S(2)}, u32[]{:S(2)}) collective-permute-start(bf16[896,768]{1,0:T(8,128)(2,1)} %add_convert_fusion.2), channel_id=1, source_target_pairs={{2,4},{3,5},{4,2},{5,3},{10,12},{11,13},{12,10},{13,11},{18,20},{1... | collective-permute-start | bytes 4128776 | tf_op jit(solution)/shard_map/ppermute | solution.py:383
  146.6 20.3 %collective-permute-start.12 = (bf16[2,512,256]{2,1,0:T(8,128)(2,1)}, bf16[2,512,256]{2,1,0:T(8,128)(2,1)S(1)}, u32[]{:S(2)}, u32[]{:S(2)}) collective-permute-start(bf16[2,512,256]{2,1,0:T(8,128)(2,1)} %get-tuple-element.86), channel_id=1, source_target_pairs={{0,2},{1,3},{2,0},{3,1},{4,6},{5,7},{6,4},{7,5},{8,10},{9,11},{10,... | collective-permute-start | bytes 1572872 | tf_op jit(solution)/shard_map/ppermute | solution.py:26
  146.8 28.1 %all-to-all-start.2 = ((bf16[4,128,2048]{2,1,0:T(8,128)(2,1)}), bf16[4,128,2048]{2,1,0:T(8,128)(2,1)S(1)}, u32[]{:S(2)}, u32[]{:S(2)}) async-start(bf16[4,128,2048]{2,1,0:T(8,128)(2,1)} %bitcast.30), calls=%async_computation.2 | async-start | bytes 4194304 | tf_op jit(solution)/shard_map/all_to_all | solution.py:359
  150.4 16.5 %copy-start.10 = (bf16[2,512,256]{2,1,0:T(8,128)(2,1)S(1)}, bf16[2,512,256]{2,1,0:T(8,128)(2,1)}, u32[]{:S(2)}) copy-start(bf16[2,512,256]{2,1,0:T(8,128)(2,1)} %get-tuple-element.96) | copy-start | bytes 1572868
  150.4 19.5 %copy-start.7 = (bf16[896,768]{1,0:T(8,128)(2,1)S(1)}, bf16[896,768]{1,0:T(8,128)(2,1)}, u32[]{:S(2)}) copy-start(bf16[896,768]{1,0:T(8,128)(2,1)} %get-tuple-element.74) | copy-start | bytes 4128772
  150.4 19.5 %copy-start.8 = (bf16[896,768]{1,0:T(8,128)(2,1)S(1)}, bf16[896,768]{1,0:T(8,128)(2,1)}, u32[]{:S(2)}) copy-start(bf16[896,768]{1,0:T(8,128)(2,1)} %get-tuple-element.90) | copy-start | bytes 4128772
  166.9 7.0 %copy-start.11 = (bf16[2,512,256]{2,1,0:T(8,128)(2,1)}, bf16[2,512,256]{2,1,0:T(8,128)(2,1)S(1)}, u32[]{:S(2)}) copy-start(bf16[2,512,256]{2,1,0:T(8,128)(2,1)S(1)} %collective-permute-done.12) | copy-start | bytes 1572868
  167.0 14.1 %collective-permute-start.15 = (bf16[512,256]{1,0:T(8,128)(2,1)S(1)}, bf16[512,256]{1,0:T(8,128)(2,1)S(1)}, u32[]{:S(2)}, u32[]{:S(2)}) collective-permute-start(bf16[512,256]{1,0:T(8,128)(2,1)S(1)} %fusion.1), channel_id=1, source_target_pairs={{0,4},{1,5},{2,6},{3,7},{4,0},{5,1},{6,2},{7,3},{8,12},{9,13},{10,... | collective-permute-start | bytes 786440 | tf_op jit(solution)/shard_map/ppermute | solution.py:26
  176.2 28.8 %all-to-all-start.1 = ((bf16[4,128,2048]{2,1,0:T(8,128)(2,1)}), bf16[4,128,2048]{2,1,0:T(8,128)(2,1)}, u32[]{:S(2)}, u32[]{:S(2)}) async-start(bf16[4,128,2048]{2,1,0:T(8,128)(2,1)} %bitcast.29), calls=%async_computation.1 | async-start | bytes 4194304 | tf_op jit(solution)/shard_map/all_to_all | solution.py:359
  181.1 29.7 %collective-permute-start.17 = (bf16[896,768]{1,0:T(8,128)(2,1)}, bf16[896,768]{1,0:T(8,128)(2,1)S(1)}, u32[]{:S(2)}, u32[]{:S(2)}) collective-permute-start(bf16[896,768]{1,0:T(8,128)(2,1)} %get-tuple-element.101), channel_id=1, source_target_pairs={{2,4},{3,5},{4,2},{5,3},{10,12},{11,13},{12,10},{13,11},{18,20},{1... | collective-permute-start | bytes 4128776 | tf_op jit(solution)/shard_map/ppermute | solution.py:383
  181.9 33.4 %collective-permute-start.18 = (bf16[896,768]{1,0:T(8,128)(2,1)}, bf16[896,768]{1,0:T(8,128)(2,1)S(1)}, u32[]{:S(2)}, u32[]{:S(2)}) collective-permute-start(bf16[896,768]{1,0:T(8,128)(2,1)} %get-tuple-element.102), channel_id=1, source_target_pairs={{0,2},{1,3},{2,0},{3,1},{4,6},{5,7},{6,4},{7,5},{8,10},{9,11},{10,... | collective-permute-start | bytes 4128776 | tf_op jit(solution)/shard_map/ppermute | solution.py:26
  187.2 1.4 collective-permute-start.16
  (5 other events, 18.3 us)
